TPU v7x, 128 devices: a whole 4x4x4 slice. The times are simulated.
128 devices in a mesh: ctx: 64 (over z, x, y_lo, core), head: 2 (over y_hi).
Axes of the slice: x: 4, y: 4 (y_hi: 2, y_lo: 2; y = y_hi * 2 + y_lo), z: 4, core: 2. Of those that a mesh axis runs over, the one named last changes fastest.
Arguments:
- frames: bfloat16 [8192, 768], P('ctx'), as said below
- tangent: bfloat16 [8192, 768], P('ctx'), may hold values from -6 to 6
- norm_gain: float32 [768], replicated, may hold values from 0.25 to 1.75
- query_weight: bfloat16 [768, 768], P(None, 'head'), as said below
- key_weight: bfloat16 [768, 768], P(None, 'head'), as said below
- value_weight: bfloat16 [768, 768], P(None, 'head'), may hold values from -0.21875 to 0.21875
- out_weight: bfloat16 [768, 768], P('head'), may hold values from -0.21875 to 0.21875
- conv_weight: float32 [31, 768], replicated, may hold values from -1 to 1
- conv_bias: float32 [768], replicated, may hold values from -3 to 3
- mix_weight: bfloat16 [768, 768], P(None, 'head'), may hold values from -0.21875 to 0.21875
Outputs:
- layer_out: bfloat16 [8192, 768], P('ctx', 'head')
- layer_slope: bfloat16 [8192, 768], P('ctx', 'head')
Inputs may be any that keep to these rules, and one draw needn't show every extreme that they name: Latent frames. `query_weight`: a projection matrix. `key_weight`: a projection matrix.
All inputs are finite; a program needn't handle non-finite values.
Results may differ from a plain program's by a relative error of at most 0.04.
The roundings to bfloat16 on the way count: a program that leaves them out, or rounds other values in their place, can miss the bound.
Values may be sent and summed in bfloat16 or wider, within the bound.
A program may use at most 128 MiB of HBM per device.

v0:
```python
import math

import jax
import jax.numpy as jnp
from jax import lax
from jax.sharding import PartitionSpec as P

HDIM = 64


epsilon = 1e-06
key_block = 1024
floor_value = -1e30


def extended(block, sides, width):
    for axis, dim in sides:
        count = lax.axis_size(axis)
        forward = [(i, i + 1) for i in range(count - 1)]
        forward.append((count - 1, 0))
        backward = [(target, source) for source, target in forward]
        low = lax.ppermute(
            lax.slice_in_dim(block, block.shape[dim] - width, None, axis=dim), axis, forward
        )
        high = lax.ppermute(lax.slice_in_dim(block, 0, width, axis=dim), axis, backward)
        block = jnp.concatenate([low, block, high], axis=dim)
    return block


def normalize(frames, tangent, norm_gain):
    plain_rows = frames.astype(jnp.float32)
    slope_rows = tangent.astype(jnp.float32)
    mean_square = jnp.mean(plain_rows * plain_rows, axis=-1, keepdims=True)
    inverse = lax.rsqrt(mean_square + epsilon)
    cross_mean = jnp.mean(plain_rows * slope_rows, axis=-1, keepdims=True)
    normed = (plain_rows * inverse * norm_gain).astype(jnp.bfloat16)
    normed_slope = (
        norm_gain * (slope_rows * inverse - plain_rows * inverse * inverse * inverse * cross_mean)
    ).astype(jnp.bfloat16)
    return (normed, normed_slope)


def split_heads(matrix):
    return matrix.reshape(matrix.shape[0], -1, HDIM)


def score_pair(queries, pair_queries, key_rows, key_slope):
    score_scale = 1.0 / math.sqrt(HDIM)
    keys_wide = split_heads(key_rows)
    pair_keys = jnp.concatenate([split_heads(key_slope), keys_wide], axis=-1)
    scores = (
        jnp.einsum("qhd,khd->hqk", queries, keys_wide, preferred_element_type=jnp.float32)
        * score_scale
    )
    slopes = (
        jnp.einsum("qhd,khd->hqk", pair_queries, pair_keys, preferred_element_type=jnp.float32)
        * score_scale
    )
    return (scores, slopes)


def weighted_sums(rounded, slanted, value_rows, value_slope):
    values_wide = split_heads(value_rows)
    summed_out = jnp.einsum(
        "hqk,khd->hqd", rounded, values_wide, preferred_element_type=jnp.float32
    )
    summed_slope = jnp.einsum(
        "hqk,khd->hqd", slanted, values_wide, preferred_element_type=jnp.float32
    ) + jnp.einsum(
        "hqk,khd->hqd", rounded, split_heads(value_slope), preferred_element_type=jnp.float32
    )
    return (summed_out, summed_slope)


def blockwise(update, running, pieces):
    row_count = pieces[0].shape[0]
    stacked = tuple(
        (
            member.reshape((row_count // key_block, key_block) + member.shape[1:])
            for member in pieces
        )
    )

    def step(inner, blocks):
        return (update(inner, blocks), None)

    running, _ = lax.scan(step, running, stacked)
    return running


def first_update(queries, pair_queries):

    def update(running, pieces):
        running_max, totals, moments = running
        scores, slopes = score_pair(queries, pair_queries, pieces[0], pieces[1])
        new_max = jnp.maximum(running_max, jnp.max(scores, axis=-1))
        shrink = jnp.exp(running_max - new_max)
        weights = jnp.exp(scores - new_max[..., None])
        return (
            new_max,
            totals * shrink + jnp.sum(weights, axis=-1),
            moments * shrink + jnp.sum(weights * slopes, axis=-1),
        )

    return update


def second_update(queries, pair_queries, running_max):

    def update(running, pieces):
        summed_out, summed_slope = running
        scores, slopes = score_pair(queries, pair_queries, pieces[0], pieces[1])
        weights = jnp.exp(scores - running_max[..., None])
        rounded = weights.astype(jnp.bfloat16)
        slanted = (weights * slopes).astype(jnp.bfloat16)
        extra_out, extra_slope = weighted_sums(rounded, slanted, pieces[2], pieces[3])
        return (summed_out + extra_out, summed_slope + extra_slope)

    return update


def conv_module(mixed, mixed_slope, tap_weights, tap_bias):
    row_count = mixed.shape[0]
    margin = tap_weights.shape[0] // 2
    stacked = jnp.stack((mixed, mixed_slope))
    padded = extended(stacked, (("ctx", 1),), margin)
    filtered = jnp.zeros(stacked.shape, jnp.float32)
    for tap_index in range(tap_weights.shape[0]):
        filtered = filtered + tap_weights[tap_index] * padded[
            :, tap_index : tap_index + row_count
        ].astype(jnp.float32)
    preact = filtered[0] + tap_bias
    gating = jax.nn.sigmoid(preact)
    active = (preact * gating).astype(jnp.bfloat16)
    active_slope = (gating * (1.0 + preact * (1.0 - gating)) * filtered[1]).astype(jnp.bfloat16)
    return (active, active_slope)


def shards(
    frames,
    tangent,
    norm_gain,
    query_weight,
    key_weight,
    value_weight,
    out_weight,
    conv_weight,
    conv_bias,
    mix_weight,
):
    row_count = frames.shape[0]
    normed, normed_slope = normalize(frames, tangent, norm_gain)

    def project(weight):
        return (
            jnp.dot(normed, weight, preferred_element_type=jnp.float32).astype(jnp.bfloat16),
            jnp.dot(normed_slope, weight, preferred_element_type=jnp.float32).astype(jnp.bfloat16),
        )

    queries, query_slope = project(query_weight)
    key_rows, key_slope = project(key_weight)
    value_rows, value_slope = project(value_weight)
    queries_wide = split_heads(queries)
    pair_queries = jnp.concatenate([queries_wide, split_heads(query_slope)], axis=-1)
    head_count = queries_wide.shape[1]
    start_max = jnp.full((head_count, row_count), floor_value, jnp.float32)
    zero_rows = jnp.zeros((head_count, row_count), jnp.float32)
    zero_sums = jnp.zeros((head_count, row_count, HDIM), jnp.float32)
    first_fn = first_update(queries_wide, pair_queries)
    running_max, totals, moments = blockwise(
        first_fn,
        (start_max, zero_rows, zero_rows),
        (
            lax.all_gather(key_rows, "ctx", axis=0, tiled=True),
            lax.all_gather(key_slope, "ctx", axis=0, tiled=True),
        ),
    )
    second_fn = second_update(queries_wide, pair_queries, running_max)
    summed_out, summed_slope = blockwise(
        second_fn,
        (zero_sums, zero_sums),
        (
            lax.all_gather(key_rows, "ctx", axis=0, tiled=True),
            lax.all_gather(key_slope, "ctx", axis=0, tiled=True),
            lax.all_gather(value_rows, "ctx", axis=0, tiled=True),
            lax.all_gather(value_slope, "ctx", axis=0, tiled=True),
        ),
    )
    attended = summed_out / totals[..., None]
    attended_slope = summed_slope / totals[..., None] - (moments / totals)[..., None] * attended
    heads_out = attended.transpose(1, 0, 2).reshape(row_count, -1).astype(jnp.bfloat16)
    heads_slope = attended_slope.transpose(1, 0, 2).reshape(row_count, -1).astype(jnp.bfloat16)
    attn_rows = jnp.dot(heads_out, out_weight, preferred_element_type=jnp.float32)
    attn_slope = jnp.dot(heads_slope, out_weight, preferred_element_type=jnp.float32)
    width = frames.shape[1]
    half_width = width // lax.axis_size("head")
    offset = lax.axis_index("head") * half_width
    attn_part, attn_part_slope = (
        lax.psum_scatter(
            attn_rows.astype(jnp.bfloat16), "head", scatter_dimension=1, tiled=True
        ).astype(jnp.float32),
        lax.psum_scatter(
            attn_slope.astype(jnp.bfloat16), "head", scatter_dimension=1, tiled=True
        ).astype(jnp.float32),
    )
    frames_part = lax.dynamic_slice_in_dim(frames, offset, half_width, 1)
    tangent_part = lax.dynamic_slice_in_dim(tangent, offset, half_width, 1)
    mixed = (frames_part.astype(jnp.float32) + attn_part).astype(jnp.bfloat16)
    mixed_slope = (tangent_part.astype(jnp.float32) + attn_part_slope).astype(jnp.bfloat16)
    tap_weights = lax.dynamic_slice_in_dim(conv_weight, offset, half_width, 1)
    tap_bias = lax.dynamic_slice_in_dim(conv_bias, offset, half_width, 0)
    active, active_slope = conv_module(mixed, mixed_slope, tap_weights, tap_bias)
    full_active, full_slope = (
        lax.all_gather(active, "head", axis=1, tiled=True),
        lax.all_gather(active_slope, "head", axis=1, tiled=True),
    )
    own_rows, own_slope = (mixed, mixed_slope)
    layer_out = (
        own_rows.astype(jnp.float32)
        + jnp.dot(full_active, mix_weight, preferred_element_type=jnp.float32)
    ).astype(jnp.bfloat16)
    layer_slope = (
        own_slope.astype(jnp.float32)
        + jnp.dot(full_slope, mix_weight, preferred_element_type=jnp.float32)
    ).astype(jnp.bfloat16)
    return (layer_out, layer_slope)


def solution(mesh):
    placed = (
        P("ctx", None),
        P("ctx", None),
        P(),
        P(None, "head"),
        P(None, "head"),
        P(None, "head"),
        P("head", None),
        P(),
        P(),
        P(None, "head"),
    )
    return jax.shard_map(
        shards,
        mesh=mesh,
        in_specs=placed,
        out_specs=(P("ctx", "head"), P("ctx", "head")),
        check_vma=False,
    )
```

profile of v0, /device:TPU:1, one launch (start us, length us, event | category | flops | bytes accessed | tf_op | source)
XLA Modules:
  0.0 648.5 jit_solution(10200798370437226867)
XLA Ops:
  17.7 105.7 %all-gather.5.cloned.1.call-done = bf16[8192,384]{1,0:T(8,128)(2,1)} async-done(((bf16[128,384]{1,0:T(8,128)(2,1)}), bf16[8192,384]{1,0:T(8,128)(2,1)}) %all-gather.5.cloned.1.call-update) | async-done | bytes 6291472 | tf_op jit(solution)/shard_map/all_gather | solution.py:183
  123.5 8.7 %copy.40 = bf16[8,1024,384]{1,2,0:T(8,128)(2,1)} copy(bf16[8,1024,384]{2,1,0:T(8,128)(2,1)} %bitcast.125) | data formatting | bytes 12582912
  132.1 101.4 %all-gather.7.cloned.1.call-done = bf16[8192,384]{1,0:T(8,128)(2,1)} async-done(((bf16[128,384]{1,0:T(8,128)(2,1)}), bf16[8192,384]{1,0:T(8,128)(2,1)}) %all-gather.7.cloned.1.call-update) | async-done | bytes 6291472 | tf_op jit(solution)/shard_map/all_gather | solution.py:184
  233.6 8.7 %copy.38 = bf16[8,1024,384]{1,2,0:T(8,128)(2,1)} copy(bf16[8,1024,384]{2,1,0:T(8,128)(2,1)} %bitcast.126) | data formatting | bytes 12582912
  242.2 61.4 %while.28 = (s32[]{:T(128)}, f32[6,128]{1,0:T(8,128)S(1)}, f32[6,128]{1,0:T(8,128)S(1)}, f32[6,128]{1,0:T(8,128)S(1)}, bf16[8,1024,384]{1,2,0:T(8,128)(2,1)}, /*...) while((s32[]{:T(128)}, f32[6,128]{1,0:T(8,128)S(1)}, ...), condition=%wide.region_6.7_spmd.clone, body=%wide.region_2.6_spmd.clone.sunk | while | flops 313005312 | bytes 27875480 | solution.py:87
  243.8 2.4 bitcast_reduce_fusion.2
  246.2 3.1 fusion.97
  251.4 2.4 bitcast_reduce_fusion.2
  253.9 3.2 fusion.97
  261.6 3.1 fusion.97
  269.2 3.2 fusion.97
  274.5 2.4 bitcast_reduce_fusion.2
  276.9 3.1 fusion.97
  282.1 2.4 bitcast_reduce_fusion.2
  284.6 3.1 fusion.97
  292.3 3.1 fusion.97
  300.0 3.1 fusion.97
  303.7 39.4 %all-gather.9.cloned.1.call-done = bf16[8192,384]{1,0:T(8,128)(2,1)} async-done(((bf16[128,384]{1,0:T(8,128)(2,1)}), bf16[8192,384]{1,0:T(8,128)(2,1)}) %all-gather.9.cloned.1.call-update) | async-done | bytes 6291472 | tf_op jit(solution)/shard_map/all_gather | solution.py:185
  343.1 109.4 %all-gather.11.cloned.1.call-done = bf16[8192,384]{1,0:T(8,128)(2,1)} async-done(((bf16[128,384]{1,0:T(8,128)(2,1)}), bf16[8192,384]{1,0:T(8,128)(2,1)}) %all-gather.11.cloned.1.call-update) | async-done | bytes 6291472 | tf_op jit(solution)/shard_map/all_gather | solution.py:186
  452.5 136.2 %while.29 = (s32[]{:T(128)}, f32[6,128,64]{1,2,0:T(8,128)S(1)}, f32[6,128,64]{1,2,0:T(8,128)S(1)}, bf16[8,1024,384]{1,2,0:T(8,128)(2,1)}, bf16[128,6,64]{0,2,1:T...) while((s32[]{:T(128)}, f32[6,128,64]{1,2,0:T(8,128)S(1)}, ...), condition=%wide.region_8.9_spmd.clone, body=%wide.region_7.8_spmd.clone.sunk | while | flops 616022016 | bytes 29795528 | solution.py:87
  459.8 2.6 convolution_add_fusion.5
  462.4 4.2 fusion.110
  466.9 2.6 fusion.111
  476.8 2.6 convolution_add_fusion.5
  479.5 4.2 fusion.110
  483.9 2.6 fusion.111
  493.9 2.6 convolution_add_fusion.5
  496.5 4.2 fusion.110
  500.9 2.6 fusion.111
  510.9 2.6 convolution_add_fusion.5
  513.5 4.2 fusion.110
  518.0 2.6 fusion.111
  527.9 2.6 convolution_add_fusion.5
  530.5 4.2 fusion.110
  535.0 2.6 fusion.111
  544.9 2.6 convolution_add_fusion.5
  547.6 4.2 fusion.110
  552.0 2.6 fusion.111
  562.0 2.6 convolution_add_fusion.5
  564.6 4.2 fusion.110
  569.0 2.6 fusion.111
  579.0 2.6 convolution_add_fusion.5
  581.6 4.2 fusion.110
  586.1 2.6 fusion.111
  591.1 12.4 %reduce-scatter.7.cloned.1.call-done = bf16[384,128]{1,0:T(8,128)(2,1)} async-done(((bf16[768,128]{1,0:T(8,128)(2,1)}), bf16[384,128]{1,0:T(8,128)(2,1)}) %reduce-scatter.7.cloned.1.call-update) | async-done | bytes 98320
  604.6 15.6 %reduce-scatter.9.cloned.1.call-done = bf16[384,128]{1,0:T(8,128)(2,1)} async-done(((bf16[768,128]{1,0:T(8,128)(2,1)}), bf16[384,128]{1,0:T(8,128)(2,1)}) %reduce-scatter.9.cloned.1.call-update) | async-done | bytes 98320
  627.3 5.6 all_gather.24
  632.9 6.9 %all_gather.25 = bf16[128,768]{1,0:T(8,128)(2,1)S(1)} all-gather(bf16[128,384]{1,0:T(8,128)(2,1)S(1)} %get-tuple-element.297), channel_id=1, replica_groups=mesh['ctx'=64,'head'=2] {'head'}, dimensions={1}, use_global_device_ids=true | all-gather | bytes 294912 | tf_op jit(solution)/shard_map/all_gather | solution.py:215
  (204 shorter events, 109.3 us)
Async XLA Ops:
  7.2 581.7 %copy-start = (bf16[384,768]{1,0:T(8,128)(2,1)S(1)}, bf16[384,768]{1,0:T(8,128)(2,1)}, u32[]{:S(2)}) copy-start(bf16[384,768]{1,0:T(8,128)(2,1)} %param.20) | copy-start | bytes 1769476
  7.2 8.2 %copy-start.2 = (bf16[128,768]{1,0:T(8,128)(2,1)S(1)}, bf16[128,768]{1,0:T(8,128)(2,1)}, u32[]{:S(2)}) copy-start(bf16[128,768]{1,0:T(8,128)(2,1)} %param.14) | copy-start | bytes 589828
  7.2 8.2 %copy-start.5 = (bf16[128,768]{1,0:T(8,128)(2,1)S(1)}, bf16[128,768]{1,0:T(8,128)(2,1)}, u32[]{:S(2)}) copy-start(bf16[128,768]{1,0:T(8,128)(2,1)} %param.15) | copy-start | bytes 589828
  7.2 8.2 %copy-start.11 = (f32[768]{0:T(1024)S(1)}, f32[768]{0:T(1024)}, u32[]{:S(2)}) copy-start(f32[768]{0:T(1024)} %param.16) | copy-start | bytes 9220
  7.2 8.2 %copy-start.7 = (bf16[768,384]{1,0:T(8,128)(2,1)S(1)}, bf16[768,384]{1,0:T(8,128)(2,1)}, u32[]{:S(2)}) copy-start(bf16[768,384]{1,0:T(8,128)(2,1)} %param.19) | copy-start | bytes 1769476
  7.2 9.4 %copy-start.8 = (bf16[768,384]{1,0:T(8,128)(2,1)S(1)}, bf16[768,384]{1,0:T(8,128)(2,1)}, u32[]{:S(2)}) copy-start(bf16[768,384]{1,0:T(8,128)(2,1)} %param.17) | copy-start | bytes 1769476
  7.2 116.2 %all-gather.5.cloned.1.call-start = ((), (), s32[]{:S(2)}) async-start(), calls=%async_computation.2 | async-start | bytes 6389760 | tf_op jit(solution)/shard_map/all_gather | solution.py:183
  10.8 222.8 %all-gather.7.cloned.1.call-start = ((), (), s32[]{:S(2)}) async-start(), calls=%async_computation.3 | async-start | bytes 6389760 | tf_op jit(solution)/shard_map/all_gather | solution.py:184
  13.2 330.0 %all-gather.9.cloned.1.call-start = ((), (), s32[]{:S(2)}) async-start(), calls=%async_computation.4 | async-start | bytes 6389760 | tf_op jit(solution)/shard_map/all_gather | solution.py:185
  15.4 437.1 %all-gather.11.cloned.1.call-start = ((), (), s32[]{:S(2)}) async-start(), calls=%async_computation.5 | async-start | bytes 6389760 | tf_op jit(solution)/shard_map/all_gather | solution.py:186
  16.5 587.1 %reduce-scatter.7.cloned.1.call-start = ((), (), s32[]{:S(2)}) async-start(), calls=%async_computation.6 | async-start | bytes 294912
  246.2 3.1 copy-start.1
  253.9 3.2 copy-start.1
  261.6 3.2 copy-start.1
  269.2 3.2 copy-start.1
  276.9 3.1 copy-start.1
  284.6 3.2 copy-start.1
  292.3 3.1 copy-start.1
  300.0 3.1 copy-start.1
  452.5 0.7 copy-start.9
  466.6 2.9 copy-start.10
  469.5 0.7 copy-start.9
  483.6 2.9 copy-start.10
  486.6 0.7 copy-start.9
  500.6 2.9 copy-start.10
  503.6 0.7 copy-start.9
  517.7 2.9 copy-start.10
  520.6 0.7 copy-start.9
  534.7 2.9 copy-start.10
  537.6 0.7 copy-start.9
  551.7 2.9 copy-start.10
  554.7 0.7 copy-start.9
  568.7 2.9 copy-start.10
  571.7 0.7 copy-start.9
  585.8 2.9 copy-start.10
  588.7 32.5 %copy-start.3 = (bf16[128,768]{1,0:T(8,128)(2,1)S(1)}, bf16[128,768]{1,0:T(8,128)(2,1)}, u32[]{:S(2)}) copy-start(bf16[128,768]{1,0:T(8,128)(2,1)} %param.14) | copy-start | bytes 589828
  588.7 32.5 %copy-start.6 = (bf16[128,768]{1,0:T(8,128)(2,1)S(1)}, bf16[128,768]{1,0:T(8,128)(2,1)}, u32[]{:S(2)}) copy-start(bf16[128,768]{1,0:T(8,128)(2,1)} %param.15) | copy-start | bytes 589828
  588.7 33.6 %copy-start.12 = (f32[768]{0:T(1024)S(1)}, f32[768]{0:T(1024)}, u32[]{:S(2)}) copy-start(f32[768]{0:T(1024)} %param.22) | copy-start | bytes 9220
  590.0 30.3 %reduce-scatter.9.cloned.1.call-start = ((), (), s32[]{:S(2)}) async-start(), calls=%async_computation.7 | async-start | bytes 294912
  621.3 3.6 collective-permute-start
  622.3 3.3 collective-permute-start.1
  625.6 14.2 %copy-start.4 = (bf16[768,384]{1,0:T(8,128)(2,1)S(1)}, bf16[768,384]{1,0:T(8,128)(2,1)}, u32[]{:S(2)}) copy-start(bf16[768,384]{1,0:T(8,128)(2,1)} %param.23) | copy-start | bytes 1769476
Sparse Core Ops, SparseCore 0:
  10.9 112.5 all-gather.4
  125.7 107.7 all-gather.6
  235.3 107.7 all-gather.8
  344.7 107.7 all-gather.10
  590.1 13.4 reduce-scatter.6
  605.8 14.3 reduce-scatter.8
where the time goes:
time: 656 us; the launch traced here: 649 us
  waiting for transfers between devices  385 us (59%)
  matrix products  150 us (23%)
  local copies, waits for them, and re-layouts  77.3 us (12%)
  between operations  14.5 us (2%)
  blocking collectives  12.6 us (2%)
  other arithmetic  7.51 us (1%)
    all_gather x1, waiting for transfers between devices, shards(): lax.all_gather(value_slope, 'ctx', axis=0, tiled=True)  109 us
    all_gather x1, waiting for transfers between devices, shards(): lax.all_gather(key_rows, 'ctx', axis=0, tiled=True)  106 us
    all_gather x1, waiting for transfers between devices, shards(): lax.all_gather(key_slope, 'ctx', axis=0, tiled=True)  101 us
    dynamic_slice x40, local copies, waits for them, and re-layouts, blockwise(): running, _ = lax.scan(step, running, stacked)  47.9 us
    all_gather x1, waiting for transfers between devices, shards(): lax.all_gather(value_rows, 'ctx', axis=0, tiled=True)  39.4 us
    dot_general x16, matrix products, score_pair(): jnp.einsum('qhd,khd->hqk', queries, keys_wide, preferred_element_type=jnp...  39 us
    dot_general x8, matrix products, weighted_sums(): jnp.einsum('hqk,khd->hqd', slanted, values_wide, preferred_element_type=j...  33.3 us
    unnamed x8, waiting for transfers between devices  28.2 us
  transfers between devices with their start and end apart: 8, of which 7 were waited for; matrix products, arithmetic and copies ran while one was open for 14% of the time, Pallas kernels for 0%

commit v1 on v0

v1 whole, which is shorter than its diff:
```python
import functools

import jax
import jax.numpy as jnp
from jax import lax
from jax.experimental import pallas as pl
from jax.experimental.pallas import tpu as pltpu
from jax.sharding import PartitionSpec as P

MESH = pl.DeviceIdType.MESH
HDIM = 64
EPSILON = 1e-06
ROWS = 128
STAT = 16
MARGIN = 16
FACTORS = {64: (4, 4, 2, 2), 8: (2, 2, 1, 2)}


def split3(value):
    first = value.astype(jnp.bfloat16)
    rest = value - first.astype(jnp.float32)
    second = rest.astype(jnp.bfloat16)
    third = (rest - second.astype(jnp.float32)).astype(jnp.bfloat16)
    return [first, second, third]


def kernel(
    sizes,
    heads,
    frames_ref,
    tangent_ref,
    gain_ref,
    wq_ref,
    wk_ref,
    wv_ref,
    wo_ref,
    taps_ref,
    bias_ref,
    wm_ref,
    out_ref,
    slope_ref,
    kv,
    qq,
    part_out,
    part_in,
    joined,
    wo_far,
    padded,
    wide,
    act,
    kv_send,
    kv_recv,
    q_send,
    q_recv,
    part_send,
    part_recv,
    head_send,
    head_recv,
    wo_sem,
    halo_sem,
    act_send,
    act_recv,
):
    zs, xs, ys, cs = sizes
    nk, nq = xs * cs, zs * ys
    count = zs * xs * ys * cs
    half = heads * HDIM
    me = lax.axis_index("ctx")
    group = lax.axis_index("head")
    core = lax.rem(me, cs)
    yl = lax.rem(me // cs, ys)
    x = lax.rem(me // (cs * ys), xs)
    z = me // (cs * ys * xs)
    my_k = x * cs + core
    my_q = z * ys + yl

    def ctx_of(z_, x_, y_, c_):
        return ((z_ * xs + x_) * ys + y_) * cs + c_

    sibling = (ctx_of(z, x, yl, 1 - core), group)
    x_peers = []
    for step in range(1, xs):
        other = lax.rem(x + step, xs)
        x_peers.append((other * cs + core, (ctx_of(z, other, yl, core), group)))

    def q_peer(offset):
        block = lax.rem(my_q + offset, nq)
        return block, (ctx_of(block // ys, x, lax.rem(block, ys), core), group)

    q_peers = [q_peer(step) for step in range(1, nq)]
    partner = (me, 1 - group)
    right = (lax.rem(me + 1, count), group)
    left = (lax.rem(me + count - 1, count), group)

    barrier = pltpu.get_barrier_semaphore()
    everyone = [sibling, partner, right, left]
    everyone += [peer for _, peer in x_peers] + [peer for _, peer in q_peers]
    for peer in everyone:
        pl.semaphore_signal(barrier, inc=1, device_id=peer, device_id_type=MESH)

    plain = frames_ref[...].astype(jnp.float32)
    slope = tangent_ref[...].astype(jnp.float32)
    gain = gain_ref[...]
    inverse = lax.rsqrt(jnp.mean(plain * plain, axis=-1, keepdims=True) + EPSILON)
    cross = jnp.mean(plain * slope, axis=-1, keepdims=True)
    normed = (plain * inverse * gain).astype(jnp.bfloat16)
    normed_slope = (
        gain * (slope * inverse - plain * inverse * inverse * inverse * cross)
    ).astype(jnp.bfloat16)
    both = jnp.concatenate([normed, normed_slope], axis=0)

    def project(weight_ref):
        return jnp.dot(both, weight_ref[...], preferred_element_type=jnp.float32)

    keys = project(wk_ref)
    low = lax.broadcasted_iota(jnp.int32, (ROWS, 2 * HDIM), 1) < HDIM
    for pair in range(heads // 2):
        cols = slice(pair * 2 * HDIM, (pair + 1) * 2 * HDIM)
        key_pair, slope_pair = keys[:ROWS, cols], keys[ROWS:, cols]
        even = jnp.where(low, key_pair, pltpu.roll(slope_pair, HDIM, 1))
        odd = jnp.where(low, pltpu.roll(key_pair, HDIM, 1), slope_pair)
        kv[2 * pair, my_k, 0] = even.astype(jnp.bfloat16)
        kv[2 * pair + 1, my_k, 0] = odd.astype(jnp.bfloat16)

    def turned(values):
        return (
            values[:ROWS].T.astype(jnp.bfloat16),
            values[ROWS:].T.astype(jnp.bfloat16),
        )

    queries, query_slope = turned(project(wq_ref))
    queries, query_slope = queries * 0.125, query_slope * 0.125
    values, value_slope = turned(project(wv_ref))
    for h in range(heads):
        rows = slice(h * HDIM, (h + 1) * HDIM)
        qq[h, my_q, :HDIM] = queries[rows]
        qq[h, my_q, HDIM:] = query_slope[rows]
        kv[h, my_k, 1, :HDIM] = values[rows]
        kv[h, my_k, 1, HDIM:] = value_slope[rows]

    pl.semaphore_wait(barrier, len(everyone))

    def kv_copy(h, block, peer):
        return pltpu.make_async_remote_copy(
            src_ref=kv.at[h, block],
            dst_ref=kv.at[h, block],
            send_sem=kv_send.at[h],
            recv_sem=kv_recv.at[h, block],
            device_id=peer,
            device_id_type=MESH,
        )

    def q_copy(h, peer):
        return pltpu.make_async_remote_copy(
            src_ref=qq.at[h, my_q],
            dst_ref=qq.at[h, my_q],
            send_sem=q_send.at[h],
            recv_sem=q_recv.at[h],
            device_id=peer,
            device_id_type=MESH,
        )

    @pl.loop(0, heads)
    def _(h):
        for _, peer in x_peers:
            kv_copy(h, my_k, peer).start()
        for _, peer in q_peers:
            q_copy(h, peer).start()
        kv_copy(h, my_k, sibling).start()

    wo_copy = pltpu.make_async_remote_copy(
        src_ref=wo_ref.at[:, pl.ds(pl.multiple_of((1 - group) * half, 128), half)],
        dst_ref=wo_far,
        send_sem=wo_sem.at[0],
        recv_sem=wo_sem.at[1],
        device_id=partner,
        device_id_type=MESH,
    )
    wo_copy.start()

    def kv_arrived(h, block):
        pltpu.make_async_copy(kv.at[h, block], kv.at[h, block], kv_recv.at[h, block]).wait()

    def forward(h):
        for block, _ in x_peers:
            kv_arrived(h, block)
            kv_copy(h, block, sibling).start()

    def part_copy(h, offset):
        block, peer = q_peer(offset)
        return pltpu.make_async_remote_copy(
            src_ref=part_out.at[h, block],
            dst_ref=part_in.at[h, my_q],
            send_sem=part_send.at[h],
            recv_sem=part_recv.at[h],
            device_id=peer,
            device_id_type=MESH,
        )

    def head_copy(h):
        here = joined.at[group, h]
        return pltpu.make_async_remote_copy(
            src_ref=here,
            dst_ref=here,
            send_sem=head_send.at[h],
            recv_sem=head_recv.at[h],
            device_id=partner,
            device_id_type=MESH,
        )

    def attend(h, tile):
        first = lax.rem(my_q + 2 * tile + 1, nq)
        second = lax.rem(my_q + 2 * tile + 2, nq)
        key_rows = kv[h, :, 0].reshape(nk * ROWS, 2 * HDIM)
        value_cols = jnp.concatenate([kv[h, b, 1] for b in range(nk)], axis=1)
        near, far = qq[h, first], qq[h, second]
        plain_q = jnp.concatenate([near[:HDIM], far[:HDIM]], axis=1)
        slope_q = jnp.concatenate([near[HDIM:], far[HDIM:]], axis=1)
        top = jnp.concatenate([plain_q, slope_q], axis=1)
        bottom = jnp.concatenate([jnp.zeros_like(plain_q), plain_q], axis=1)
        product = jnp.dot(
            key_rows, jnp.concatenate([top, bottom], axis=0), preferred_element_type=jnp.float32
        )
        width = 2 * ROWS
        scores, slopes = product[:, :width], product[:, width:]
        peak = jnp.max(scores, axis=0, keepdims=True)
        weights = jnp.exp(scores - peak)
        slanted = weights * slopes
        totals = jnp.sum(weights, axis=0, keepdims=True)
        moments = jnp.sum(slanted, axis=0, keepdims=True)
        stacked = jnp.concatenate(
            [weights.astype(jnp.bfloat16), slanted.astype(jnp.bfloat16)], axis=1
        )
        sums = jnp.dot(value_cols, stacked, preferred_element_type=jnp.float32)
        share = 1.0 / totals
        center = moments * share
        attended = sums[:HDIM, :width] * share
        tilted = (sums[HDIM:, :width] + sums[:HDIM, width:]) * share - center * attended
        stats = split3(peak + jnp.log(totals)) + split3(center)
        stats = jnp.concatenate(
            [s.astype(jnp.float32) for s in stats]
            + [jnp.zeros((STAT - len(stats), width), jnp.float32)],
            axis=0,
        ).astype(jnp.bfloat16)
        attended, tilted = attended.astype(jnp.bfloat16), tilted.astype(jnp.bfloat16)
        for place, block in enumerate((first, second)):
            cols = slice(place * ROWS, (place + 1) * ROWS)
            part_out[h, block, :HDIM] = attended[:, cols]
            part_out[h, block, HDIM : 2 * HDIM] = tilted[:, cols]
            part_out[h, block, 2 * HDIM :] = stats[:, cols]

    def combine(h):
        part_in[h, my_q] = part_out[h, my_q]
        landed = part_in.at[h, pl.ds(0, nq - 1)]
        pltpu.make_async_copy(landed, landed, part_recv.at[h]).wait()
        logs, centers = [], []
        for b in range(nq):
            stats = part_in[h, b, 2 * HDIM :].astype(jnp.float32)
            logs.append(stats[0:1] + stats[1:2] + stats[2:3])
            centers.append(stats[3:4] + stats[4:5] + stats[5:6])
        top = functools.reduce(jnp.maximum, logs)
        shares = [jnp.exp(entry - top) for entry in logs]
        scale = 1.0 / functools.reduce(jnp.add, shares)
        shares = [entry * scale for entry in shares]
        middle = functools.reduce(jnp.add, [s * c for s, c in zip(shares, centers)])
        attended = jnp.zeros((HDIM, ROWS), jnp.float32)
        tilted = jnp.zeros((HDIM, ROWS), jnp.float32)
        for b in range(nq):
            piece = part_in[h, b, :HDIM].astype(jnp.float32) * shares[b]
            attended = attended + piece
            tilted = tilted + part_in[h, b, HDIM : 2 * HDIM].astype(jnp.float32) * shares[b]
            tilted = tilted + piece * (centers[b] - middle)
        joined[group, h, :HDIM] = attended.astype(jnp.bfloat16)
        joined[group, h, HDIM:] = tilted.astype(jnp.bfloat16)
        head_copy(h).start()

    forward(0)

    @pl.loop(0, heads)
    def _(h):
        for step in range(xs):
            kv_arrived(h, lax.rem(x + step, xs) * cs + 1 - core)
        landed = qq.at[h, pl.ds(0, nq - 1)]
        pltpu.make_async_copy(landed, landed, q_recv.at[h]).wait()

        @pl.loop(0, nq // 2)
        def _(tile):
            attend(h, tile)
            part_copy(h, 2 * tile + 1).start()

            @pl.when(tile < nq // 2 - 1)
            def _():
                part_copy(h, 2 * tile + 2).start()

            @pl.when(jnp.logical_and(tile == 0, h < heads - 1))
            def _():
                forward(h + 1)

        @pl.when(h >= 2)
        def _():
            combine(h - 2)

    for h in range(max(heads - 2, 0), heads):
        combine(h)

    wo_copy.wait()
    for h in range(heads):
        head_copy(h).wait()

    offset = pl.multiple_of(group * half, 128)
    own_cols = pl.ds(offset, half)

    def rows_of(source, lower):
        stacked = joined[source, :, lower : lower + HDIM].reshape(half, ROWS)
        return stacked.astype(jnp.float32).T.astype(jnp.bfloat16)

    def heads_of(source):
        return jnp.concatenate([rows_of(source, 0), rows_of(source, HDIM)], axis=0)

    mixing = jnp.dot(heads_of(group), wo_ref[:, own_cols], preferred_element_type=jnp.float32)
    mixing += jnp.dot(heads_of(1 - group), wo_far[...], preferred_element_type=jnp.float32)
    padded[0, MARGIN : MARGIN + ROWS] = (
        frames_ref[:, own_cols].astype(jnp.float32) + mixing[:ROWS]
    ).astype(jnp.bfloat16)
    padded[1, MARGIN : MARGIN + ROWS] = (
        tangent_ref[:, own_cols].astype(jnp.float32) + mixing[ROWS:]
    ).astype(jnp.bfloat16)

    to_right = pltpu.make_async_remote_copy(
        src_ref=padded.at[:, pl.ds(ROWS, MARGIN)],
        dst_ref=padded.at[:, pl.ds(0, MARGIN)],
        send_sem=halo_sem.at[0],
        recv_sem=halo_sem.at[1],
        device_id=right,
        device_id_type=MESH,
    )
    to_left = pltpu.make_async_remote_copy(
        src_ref=padded.at[:, pl.ds(MARGIN, MARGIN)],
        dst_ref=padded.at[:, pl.ds(ROWS + MARGIN, MARGIN)],
        send_sem=halo_sem.at[2],
        recv_sem=halo_sem.at[3],
        device_id=left,
        device_id_type=MESH,
    )
    to_right.start()
    to_left.start()
    to_right.wait()
    to_left.wait()
    wide[...] = padded[...].astype(jnp.float32)

    taps = taps_ref.shape[0]
    reach = MARGIN - taps // 2

    def act_copy(chunk):
        here = act.at[group, chunk]
        return pltpu.make_async_remote_copy(
            src_ref=here,
            dst_ref=here,
            send_sem=act_send.at[chunk],
            recv_sem=act_recv.at[chunk],
            device_id=partner,
            device_id_type=MESH,
        )

    chunks = half // 128
    for chunk in range(chunks):
        cols = slice(chunk * 128, (chunk + 1) * 128)
        far_cols = pl.ds(pl.multiple_of(offset + chunk * 128, 128), 128)
        weights = taps_ref[:, far_cols]
        filtered = []
        for which in range(2):
            total = jnp.zeros((ROWS, 128), jnp.float32)
            for phase in range(8):
                partial = None
                for tap in range(phase, taps, 8):
                    start = tap - phase
                    term = weights[tap : tap + 1] * wide[which, start : start + ROWS + 8, cols]
                    partial = term if partial is None else partial + term
                total = total + partial[phase + reach : phase + reach + ROWS]
            filtered.append(total)
        preact = filtered[0] + bias_ref[:, far_cols]
        gating = 1.0 / (1.0 + jnp.exp(-preact))
        act[group, chunk, 0] = (preact * gating).astype(jnp.bfloat16)
        act[group, chunk, 1] = (
            gating * (1.0 + preact * (1.0 - gating)) * filtered[1]
        ).astype(jnp.bfloat16)
        act_copy(chunk).start()

    def mix(source):
        rows = jnp.concatenate(
            [act[source, chunk].reshape(2 * ROWS, 128) for chunk in range(chunks)], axis=1
        )
        weight = wm_ref[pl.ds(pl.multiple_of(source * half, 128), half), :]
        return jnp.dot(rows, weight, preferred_element_type=jnp.float32)

    total = mix(group)
    for chunk in range(chunks):
        act_copy(chunk).wait()
    total = total + mix(1 - group)
    out_ref[...] = (wide[0, MARGIN : MARGIN + ROWS] + total[:ROWS]).astype(jnp.bfloat16)
    slope_ref[...] = (wide[1, MARGIN : MARGIN + ROWS] + total[ROWS:]).astype(jnp.bfloat16)

    @pl.loop(0, heads)
    def _(h):
        sent = kv.at[h, pl.ds(0, xs - 1 + 1 + xs - 1)]
        pltpu.make_async_copy(sent, sent, kv_send.at[h]).wait()
        sent = qq.at[h, pl.ds(0, nq - 1)]
        pltpu.make_async_copy(sent, sent, q_send.at[h]).wait()
        sent = part_out.at[h, pl.ds(0, nq - 1)]
        pltpu.make_async_copy(sent, sent, part_send.at[h]).wait()


def shards(
    sizes,
    frames,
    tangent,
    norm_gain,
    query_weight,
    key_weight,
    value_weight,
    out_weight,
    conv_weight,
    conv_bias,
    mix_weight,
):
    zs, xs, ys, cs = sizes
    nk, nq = xs * cs, zs * ys
    half = query_weight.shape[1]
    heads = half // HDIM
    sem = pltpu.SemaphoreType.DMA
    vmem = pl.BlockSpec(memory_space=pltpu.VMEM)
    shape = jax.ShapeDtypeStruct((ROWS, half), jnp.bfloat16)
    return pl.pallas_call(
        functools.partial(kernel, sizes, heads),
        out_shape=(shape, shape),
        in_specs=[vmem] * 10,
        out_specs=(vmem, vmem),
        scratch_shapes=[
            pltpu.VMEM((heads, nk, 2, ROWS, 2 * HDIM), jnp.bfloat16),
            pltpu.VMEM((heads, nq, 2 * HDIM, ROWS), jnp.bfloat16),
            pltpu.VMEM((heads, nq, 2 * HDIM + STAT, ROWS), jnp.bfloat16),
            pltpu.VMEM((heads, nq, 2 * HDIM + STAT, ROWS), jnp.bfloat16),
            pltpu.VMEM((2, heads, 2 * HDIM, ROWS), jnp.bfloat16),
            pltpu.VMEM((half, half), jnp.bfloat16),
            pltpu.VMEM((2, ROWS + 2 * MARGIN, half), jnp.bfloat16),
            pltpu.VMEM((2, ROWS + 2 * MARGIN, half), jnp.float32),
            pltpu.VMEM((2, half // 128, 2, ROWS, 128), jnp.bfloat16),
            sem((heads,)),
            sem((heads, nk)),
            sem((heads,)),
            sem((heads,)),
            sem((heads,)),
            sem((heads,)),
            sem((heads,)),
            sem((heads,)),
            sem((2,)),
            sem((4,)),
            sem((half // 128,)),
            sem((half // 128,)),
        ],
        compiler_params=pltpu.CompilerParams(
            collective_id=0, has_side_effects=True, vmem_limit_bytes=48 * 1024 * 1024
        ),
        name="block",
    )(
        frames,
        tangent,
        norm_gain.reshape(1, -1),
        query_weight,
        key_weight,
        value_weight,
        out_weight,
        conv_weight,
        conv_bias.reshape(1, -1),
        mix_weight,
    )


def solution(mesh):
    sizes = FACTORS[mesh.shape["ctx"]]
    placed = (
        P("ctx", None),
        P("ctx", None),
        P(),
        P(None, "head"),
        P(None, "head"),
        P(None, "head"),
        P("head", None),
        P(),
        P(),
        P(None, "head"),
    )
    return jax.shard_map(
        functools.partial(shards, sizes),
        mesh=mesh,
        in_specs=placed,
        out_specs=(P("ctx", "head"), P("ctx", "head")),
        check_vma=False,
    )
```

time: 656 us -> 80.5 us (0.12); the launches traced: 649 us -> 80.1 us
  waiting for transfers between devices: 385 us -> 0 us
  matrix products: 150 us -> 0 us
  Pallas kernels: 0 us -> 69.4 us
  local copies, waits for them, and re-layouts: 77.3 us -> 10 us
  between operations: 14.5 us -> 0.67 us
  blocking collectives: 12.6 us -> 0 us
  other arithmetic: 7.51 us -> 0 us
    all_gather x4 -> x0, waiting for transfers between devices: 356 us -> none  [the longest x1 109 us: shards(): lax.all_gather(value_slope, 'ctx', axis=0, tiled=True)]
    dot_general x58 -> x0, matrix products: 150 us -> none  [the longest x16 39 us: score_pair(): jnp.einsum('qhd,khd->hqk', queries, keys_wide, preferred_element_type=jnp...]
    pallas_call x0 -> x1, Pallas kernels: none -> 69.4 us  [shards(): pl.pallas_call(functools.partial(kernel, sizes, heads), out_shape=(shape,...]
    dynamic_slice x41 -> x0, local copies, waits for them, and re-layouts: 48 us -> none  [the longest x40 47.9 us: blockwise(): running, _ = lax.scan(step, running, stacked)]
    unnamed x8 -> x0, waiting for transfers between devices: 28.2 us -> none
    all_gather x2 -> x0, blocking collectives: 12.6 us -> none  [the longest x1 6.93 us: shards(): lax.all_gather(active_slope, 'head', axis=1, tiled=True)]
    unnamed x27 -> x20, local copies, waits for them, and re-layouts: 21.2 us -> 9.35 us
  transfers between devices with their start and end apart: 8 -> 0, of which waited for: 7 -> 0; matrix products, arithmetic and copies ran while one was open for 14% -> 0% of each run, Pallas kernels for 0% -> 0%
where the time goes in v1:
time: 80.5 us; the launch traced here: 80.1 us
  Pallas kernels  69.4 us (86%)
  local copies, waits for them, and re-layouts  10 us (12%)
    pallas_call x1, Pallas kernels, shards(): pl.pallas_call(functools.partial(kernel, sizes, heads), out_shape=(shape,...  69.4 us
    unnamed x20, local copies, waits for them, and re-layouts  9.35 us

profile of v1, /device:TPU:1, one launch (start us, length us, event | category | flops | bytes accessed | tf_op | source)
XLA Modules:
  0.0 80.1 jit_solution(4638827220361301637)
XLA Ops:
  0.6 0.0 copy-start.8
  0.6 0.7 reshape.10.gain_ref
  1.3 0.0 copy-done.8
  1.3 0.0 copy-start
  1.4 1.1 %copy-done = bf16[768,384]{1,0:T(8,128)(2,1)S(1)} copy-done((bf16[768,384]{1,0:T(8,128)(2,1)S(1)}, bf16[768,384]{1,0:T(8,128)(2,1)}, u32[]{:S(2)}) %copy-start) | copy-done | bytes 589848
  2.4 0.0 copy-start.1
  2.4 1.1 %copy-done.1 = bf16[768,384]{1,0:T(8,128)(2,1)S(1)} copy-done((bf16[768,384]{1,0:T(8,128)(2,1)S(1)}, bf16[768,384]{1,0:T(8,128)(2,1)}, u32[]{:S(2)}) %copy-start.1) | copy-done | bytes 589848
  3.5 0.0 copy-start.2
  3.5 1.1 %copy-done.2 = bf16[768,384]{1,0:T(8,128)(2,1)S(1)} copy-done((bf16[768,384]{1,0:T(8,128)(2,1)S(1)}, bf16[768,384]{1,0:T(8,128)(2,1)}, u32[]{:S(2)}) %copy-start.2) | copy-done | bytes 589848
  4.5 0.0 copy-start.3
  4.5 1.1 %copy-done.3 = bf16[384,768]{1,0:T(8,128)(2,1)S(1)} copy-done((bf16[384,768]{1,0:T(8,128)(2,1)S(1)}, bf16[384,768]{1,0:T(8,128)(2,1)}, u32[]{:S(2)}) %copy-start.3) | copy-done | bytes 589848
  5.6 0.0 copy-start.4
  5.6 1.1 %copy-done.4 = bf16[768,384]{1,0:T(8,128)(2,1)S(1)} copy-done((bf16[768,384]{1,0:T(8,128)(2,1)S(1)}, bf16[768,384]{1,0:T(8,128)(2,1)}, u32[]{:S(2)}) %copy-start.4) | copy-done | bytes 589848
  6.7 0.0 copy-start.5
  6.7 0.9 %copy-done.5 = bf16[128,768]{1,0:T(8,128)(2,1)S(1)} copy-done((bf16[128,768]{1,0:T(8,128)(2,1)S(1)}, bf16[128,768]{1,0:T(8,128)(2,1)}, u32[]{:S(2)}) %copy-start.5) | copy-done | bytes 196632
  7.6 0.0 copy-start.6
  7.6 0.9 %copy-done.6 = bf16[128,768]{1,0:T(8,128)(2,1)S(1)} copy-done((bf16[128,768]{1,0:T(8,128)(2,1)S(1)}, bf16[128,768]{1,0:T(8,128)(2,1)}, u32[]{:S(2)}) %copy-start.6) | copy-done | bytes 196632
  8.5 0.0 copy-start.7
  8.5 0.9 %copy-done.7 = f32[31,768]{1,0:T(8,128)S(1)} copy-done((f32[31,768]{1,0:T(8,128)S(1)}, f32[31,768]{1,0:T(8,128)}, u32[]{:S(2)}) %copy-start.7) | copy-done | bytes 95256
  9.4 69.4 %block.1 = (bf16[128,384]{1,0:T(8,128)(2,1)S(1)}, bf16[128,384]{1,0:T(8,128)(2,1)S(1)}) custom-call(bf16[128,768]{1,0:T(8,128)(2,1)S(1)} %copy-done.5, bf16[128,768]{1,0:T(8,128)(2,1)S(1)} %copy-done.6, f32[1,768]{1,0:T(1,128)S(1)} %reshape.10.gain_ref, bf16[768,384]{1,0:T(8,128)(2,1)S(1)} %copy-done, bf16[768,384]{1,0:T(8,128)(2,1)S(1)} %copy-done.1, ...), custom_call_target="tpu_custom_call" | custom-call | tf_op jit(solution)/shard_map/block/pallas_call | solution.py:433
  78.8 0.6 copy.14
  79.4 0.6 copy.15
  (1 shorter events, 0.0 us)
Async XLA Ops:
  0.6 0.7 copy-start.8
  1.3 1.1 %copy-start = (bf16[768,384]{1,0:T(8,128)(2,1)S(1)}, bf16[768,384]{1,0:T(8,128)(2,1)}, u32[]{:S(2)}) copy-start(bf16[768,384]{1,0:T(8,128)(2,1)} %wq_ref.1) | copy-start | bytes 1769476
  2.4 1.1 %copy-start.1 = (bf16[768,384]{1,0:T(8,128)(2,1)S(1)}, bf16[768,384]{1,0:T(8,128)(2,1)}, u32[]{:S(2)}) copy-start(bf16[768,384]{1,0:T(8,128)(2,1)} %wk_ref.1) | copy-start | bytes 1769476
  3.5 1.1 %copy-start.2 = (bf16[768,384]{1,0:T(8,128)(2,1)S(1)}, bf16[768,384]{1,0:T(8,128)(2,1)}, u32[]{:S(2)}) copy-start(bf16[768,384]{1,0:T(8,128)(2,1)} %wv_ref.1) | copy-start | bytes 1769476
  4.5 1.1 %copy-start.3 = (bf16[384,768]{1,0:T(8,128)(2,1)S(1)}, bf16[384,768]{1,0:T(8,128)(2,1)}, u32[]{:S(2)}) copy-start(bf16[384,768]{1,0:T(8,128)(2,1)} %wo_ref.1) | copy-start | bytes 1769476
  5.6 1.1 %copy-start.4 = (bf16[768,384]{1,0:T(8,128)(2,1)S(1)}, bf16[768,384]{1,0:T(8,128)(2,1)}, u32[]{:S(2)}) copy-start(bf16[768,384]{1,0:T(8,128)(2,1)} %wm_ref.1) | copy-start | bytes 1769476
  6.7 0.9 %copy-start.5 = (bf16[128,768]{1,0:T(8,128)(2,1)S(1)}, bf16[128,768]{1,0:T(8,128)(2,1)}, u32[]{:S(2)}) copy-start(bf16[128,768]{1,0:T(8,128)(2,1)} %frames_ref.1) | copy-start | bytes 589828
  7.6 0.9 %copy-start.6 = (bf16[128,768]{1,0:T(8,128)(2,1)S(1)}, bf16[128,768]{1,0:T(8,128)(2,1)}, u32[]{:S(2)}) copy-start(bf16[128,768]{1,0:T(8,128)(2,1)} %tangent_ref.1) | copy-start | bytes 589828
  8.5 0.9 %copy-start.7 = (f32[31,768]{1,0:T(8,128)S(1)}, f32[31,768]{1,0:T(8,128)}, u32[]{:S(2)}) copy-start(f32[31,768]{1,0:T(8,128)} %taps_ref.1) | copy-start | bytes 285700

commit v2 on v1

v2 whole, which is shorter than its diff:
```python
import functools

import jax
import jax.numpy as jnp
from jax import lax
from jax.experimental import pallas as pl
from jax.experimental.pallas import tpu as pltpu
from jax.sharding import PartitionSpec as P

MESH = pl.DeviceIdType.MESH
HDIM = 64
EPSILON = 1e-06
ROWS = 128
STAT = 16
MARGIN = 16
FACTORS = {64: (4, 4, 2, 2)}


def split3(value):
    first = value.astype(jnp.bfloat16)
    rest = value - first.astype(jnp.float32)
    second = rest.astype(jnp.bfloat16)
    third = (rest - second.astype(jnp.float32)).astype(jnp.bfloat16)
    return [first, second, third]


def kernel(
    sizes,
    heads,
    frames_hbm,
    tangent_hbm,
    gain_hbm,
    wq_hbm,
    wk_hbm,
    wv_hbm,
    wo_hbm,
    taps_hbm,
    bias_hbm,
    wm_hbm,
    out_ref,
    slope_ref,
    frames_ref,
    tangent_ref,
    gain_ref,
    wq_ref,
    wk_ref,
    wv_ref,
    wo_ref,
    taps_ref,
    bias_ref,
    wm_ref,
    stage_kv,
    stage_q,
    kv,
    qq,
    part_out,
    part_in,
    merged,
    joined,
    wo_far,
    padded,
    wide,
    act,
    load_sem,
    relay_sem,
    relay_q_sem,
    kv_send,
    direct_recv,
    sibling_recv,
    q_send,
    q_recv,
    part_send,
    part_recv,
    head_send,
    head_recv,
    wo_sem,
    halo_sem,
    act_send,
    act_recv,
):
    zs, xs, ys, cs = sizes
    count = zs * xs * ys * cs
    half = heads * HDIM
    own = heads // ys
    nk = xs * cs * ys
    span = ys * ROWS
    me = lax.axis_index("ctx")
    group = lax.axis_index("head")
    core = lax.rem(me, cs)
    yl = lax.rem(me // cs, ys)
    x = lax.rem(me // (cs * ys), xs)
    z = me // (cs * ys * xs)

    def ctx_of(z_, x_, y_, c_):
        return ((z_ * xs + x_) * ys + y_) * cs + c_

    sibling = (ctx_of(z, x, yl, 1 - core), group)
    fellow = (ctx_of(z, x, 1 - yl, core), group)
    partner = (me, 1 - group)
    diagonal = (ctx_of(z, x, 1 - yl, core), 1 - group)
    right = (lax.rem(me + 1, count), group)
    left = (lax.rem(me + count - 1, count), group)
    x_peers = []
    for step in range(1, xs):
        other = lax.rem(x + step, xs)
        x_peers.append((other, (ctx_of(z, other, yl, core), group)))

    def z_peer(step):
        other = lax.rem(z + step, zs)
        return other, (ctx_of(other, x, yl, core), group)

    z_peers = [z_peer(step) for step in range(1, zs)]

    loads = []
    for source, target in (
        (frames_hbm, frames_ref),
        (tangent_hbm, tangent_ref),
        (gain_hbm, gain_ref),
        (wk_hbm, wk_ref),
        (wv_hbm, wv_ref),
        (wq_hbm, wq_ref),
        (wo_hbm, wo_ref),
        (wm_hbm, wm_ref),
        (taps_hbm, taps_ref),
        (bias_hbm, bias_ref),
    ):
        load = pltpu.make_async_copy(source, target, load_sem.at[len(loads)])
        load.start()
        loads.append(load)

    barrier = pltpu.get_barrier_semaphore()
    everyone = [sibling, fellow, partner, diagonal, right, left]
    everyone += [peer for _, peer in x_peers] + [peer for _, peer in z_peers]
    for peer in everyone:
        pl.semaphore_signal(barrier, inc=1, device_id=peer, device_id_type=MESH)

    def send(source, target, send_sem, recv_sem, peer):
        return pltpu.make_async_remote_copy(
            src_ref=source,
            dst_ref=target,
            send_sem=send_sem,
            recv_sem=recv_sem,
            device_id=peer,
            device_id_type=MESH,
        )

    def drain(ref, sem):
        pltpu.make_async_copy(ref, ref, sem).wait()

    for load in loads[:3]:
        load.wait()
    plain = frames_ref[...].astype(jnp.float32)
    slope = tangent_ref[...].astype(jnp.float32)
    gain = gain_ref[...]
    inverse = lax.rsqrt(jnp.mean(plain * plain, axis=-1, keepdims=True) + EPSILON)
    cross = jnp.mean(plain * slope, axis=-1, keepdims=True)
    normed = (plain * inverse * gain).astype(jnp.bfloat16)
    normed_slope = (
        gain * (slope * inverse - plain * inverse * inverse * inverse * cross)
    ).astype(jnp.bfloat16)
    both = jnp.concatenate([normed, normed_slope], axis=0)

    def project(weight_ref):
        return jnp.dot(both, weight_ref[...], preferred_element_type=jnp.float32)

    loads[3].wait()
    keys = project(wk_ref)
    low = lax.broadcasted_iota(jnp.int32, (ROWS, 2 * HDIM), 1) < HDIM
    for pair in range(heads // 2):
        cols = slice(pair * 2 * HDIM, (pair + 1) * 2 * HDIM)
        key_pair, slope_pair = keys[:ROWS, cols], keys[ROWS:, cols]
        even = jnp.where(low, key_pair, pltpu.roll(slope_pair, HDIM, 1))
        odd = jnp.where(low, pltpu.roll(key_pair, HDIM, 1), slope_pair)
        for h, value in ((2 * pair, even), (2 * pair + 1, odd)):
            stage_kv[h // own, h % own, 0] = value.astype(jnp.bfloat16)

    def turned(values):
        return (
            values[:ROWS].T.astype(jnp.bfloat16),
            values[ROWS:].T.astype(jnp.bfloat16),
        )

    loads[4].wait()
    values, value_slope = turned(project(wv_ref))
    loads[5].wait()
    queries, query_slope = turned(project(wq_ref))
    queries, query_slope = queries * 0.125, query_slope * 0.125
    for h in range(heads):
        rows = slice(h * HDIM, (h + 1) * HDIM)
        stage_kv[h // own, h % own, 1, :HDIM] = values[rows]
        stage_kv[h // own, h % own, 1, HDIM:] = value_slope[rows]
        stage_q[h // own, h % own, :HDIM] = queries[rows]
        stage_q[h // own, h % own, HDIM:] = query_slope[rows]

    pl.semaphore_wait(barrier, len(everyone))

    def slot(x_, c_, y_):
        return (x_ * cs + c_) * ys + y_

    def relay_kv(j):
        return send(
            stage_kv.at[1 - yl, j],
            kv.at[j, slot(x, core, yl)],
            relay_sem.at[0, j],
            relay_sem.at[1, j],
            fellow,
        )

    def relay_q(j):
        return send(
            stage_q.at[1 - yl, j],
            qq.at[j, z * ys + yl],
            relay_q_sem.at[0, j],
            relay_q_sem.at[1, j],
            fellow,
        )

    def direct(j, which, peer):
        here = kv.at[j, slot(x, core, which)]
        return send(here, here, kv_send.at[j], direct_recv.at[j, x, which], peer)

    def pass_on(j, source):
        here = kv.at[j, pl.ds(slot(source, core, 0), ys)]
        return send(here, here, kv_send.at[j], sibling_recv.at[j, source], sibling)

    for j in range(own):
        relay_kv(j).start()
        relay_q(j).start()
        kv[j, slot(x, core, yl)] = stage_kv[yl, j]
        qq[j, z * ys + yl] = stage_q[yl, j]
        for _, peer in x_peers:
            direct(j, yl, peer).start()

    def relay(j):
        relay_kv(j).wait()
        for _, peer in x_peers:
            direct(j, 1 - yl, peer).start()
        pass_on(j, x).start()
        relay_q(j).wait()
        here = qq.at[j, pl.ds(z * ys, ys)]
        for _, peer in z_peers:
            send(here, here, q_send.at[j], q_recv.at[j], peer).start()

    def forward(j):
        for other, _ in x_peers:
            for which in range(ys):
                drain(kv.at[j, slot(other, core, which)], direct_recv.at[j, other, which])
            pass_on(j, other).start()

    relay(0)
    relay(1)
    loads[6].wait()
    wo_copy = send(
        wo_ref.at[:, pl.ds(pl.multiple_of((1 - group) * half, 128), half)],
        wo_far,
        wo_sem.at[0],
        wo_sem.at[1],
        partner,
    )
    wo_copy.start()
    forward(0)
    for j in range(2, own):
        relay(j)

    def attend(j, other):
        key_rows = kv[j, :, 0].reshape(nk * ROWS, 2 * HDIM)
        value_cols = jnp.concatenate([kv[j, b, 1] for b in range(nk)], axis=1)
        blocks = [qq[j, other * ys + y] for y in range(ys)]
        plain_q = jnp.concatenate([block[:HDIM] for block in blocks], axis=1)
        slope_q = jnp.concatenate([block[HDIM:] for block in blocks], axis=1)
        top = jnp.concatenate([plain_q, slope_q], axis=1)
        bottom = jnp.concatenate([jnp.zeros_like(plain_q), plain_q], axis=1)
        product = jnp.dot(
            key_rows, jnp.concatenate([top, bottom], axis=0), preferred_element_type=jnp.float32
        )
        scores, slopes = product[:, :span], product[:, span:]
        peak = jnp.max(scores, axis=0, keepdims=True)
        weights = jnp.exp(scores - peak)
        slanted = weights * slopes
        totals = jnp.sum(weights, axis=0, keepdims=True)
        moments = jnp.sum(slanted, axis=0, keepdims=True)
        stacked = jnp.concatenate(
            [weights.astype(jnp.bfloat16), slanted.astype(jnp.bfloat16)], axis=1
        )
        sums = jnp.dot(value_cols, stacked, preferred_element_type=jnp.float32)
        share = 1.0 / totals
        center = moments * share
        attended = sums[:HDIM, :span] * share
        tilted = (sums[HDIM:, :span] + sums[:HDIM, span:]) * share - center * attended
        stats = split3(peak + jnp.log(totals)) + split3(center)
        stats = jnp.concatenate(
            [s.astype(jnp.float32) for s in stats]
            + [jnp.zeros((STAT - len(stats), span), jnp.float32)],
            axis=0,
        )
        part_out[j, other, :HDIM] = attended.astype(jnp.bfloat16)
        part_out[j, other, HDIM : 2 * HDIM] = tilted.astype(jnp.bfloat16)
        part_out[j, other, 2 * HDIM :] = stats.astype(jnp.bfloat16)

    def combine(j):
        part_in[j, z] = part_out[j, z]
        if zs > 1:
            drain(part_in.at[j, pl.ds(0, zs - 1)], part_recv.at[j])
        logs, centers = [], []
        for b in range(zs):
            stats = part_in[j, b, 2 * HDIM :].astype(jnp.float32)
            logs.append(stats[0:1] + stats[1:2] + stats[2:3])
            centers.append(stats[3:4] + stats[4:5] + stats[5:6])
        top = functools.reduce(jnp.maximum, logs)
        shares = [jnp.exp(entry - top) for entry in logs]
        scale = 1.0 / functools.reduce(jnp.add, shares)
        shares = [entry * scale for entry in shares]
        middle = functools.reduce(jnp.add, [s * c for s, c in zip(shares, centers)])
        attended = jnp.zeros((HDIM, span), jnp.float32)
        tilted = jnp.zeros((HDIM, span), jnp.float32)
        for b in range(zs):
            piece = part_in[j, b, :HDIM].astype(jnp.float32) * shares[b]
            attended = attended + piece
            tilted = tilted + part_in[j, b, HDIM : 2 * HDIM].astype(jnp.float32) * shares[b]
            tilted = tilted + piece * (centers[b] - middle)
        result = jnp.concatenate([attended, tilted], axis=0).astype(jnp.bfloat16)
        for y in range(ys):
            merged[j, y] = result[:, y * ROWS : (y + 1) * ROWS]
        here = joined.at[group, yl, j]
        for peer, row_block in ((fellow, 1 - yl), (diagonal, 1 - yl), (partner, yl)):
            send(merged.at[j, row_block], here, head_send.at[j], head_recv.at[j], peer).start()
        joined[group, yl, j] = merged[j, yl]

    @pl.loop(0, own)
    def _(j):
        for step in range(xs):
            source = lax.rem(x + step, xs)
            drain(
                kv.at[j, pl.ds(slot(source, 1 - core, 0), ys)], sibling_recv.at[j, source]
            )
        if zs > 1:
            drain(qq.at[j, pl.ds(0, ys * (zs - 1))], q_recv.at[j])

        @pl.loop(0, zs)
        def _(tile):
            other, peer = z_peer(tile + 1)
            attend(j, other)

            @pl.when(tile < zs - 1)
            def _():
                send(
                    part_out.at[j, other],
                    part_in.at[j, z],
                    part_send.at[j],
                    part_recv.at[j],
                    peer,
                ).start()

            @pl.when(jnp.logical_and(tile == 0, j < own - 1))
            def _():
                forward(j + 1)

        @pl.when(j >= 1)
        def _():
            combine(j - 1)

    combine(own - 1)

    wo_copy.wait()
    for j in range(own):
        drain(joined.at[0, 0, pl.ds(0, 3)], head_recv.at[j])

    offset = pl.multiple_of(group * half, 128)
    own_cols = pl.ds(offset, half)

    def rows_of(source, lower):
        stacked = joined[source, :, :, lower : lower + HDIM].reshape(half, ROWS)
        return stacked.astype(jnp.float32).T.astype(jnp.bfloat16)

    def heads_of(source):
        return jnp.concatenate([rows_of(source, 0), rows_of(source, HDIM)], axis=0)

    mixing = jnp.dot(heads_of(group), wo_ref[:, own_cols], preferred_element_type=jnp.float32)
    mixing += jnp.dot(heads_of(1 - group), wo_far[...], preferred_element_type=jnp.float32)
    padded[0, MARGIN : MARGIN + ROWS] = (
        frames_ref[:, own_cols].astype(jnp.float32) + mixing[:ROWS]
    ).astype(jnp.bfloat16)
    padded[1, MARGIN : MARGIN + ROWS] = (
        tangent_ref[:, own_cols].astype(jnp.float32) + mixing[ROWS:]
    ).astype(jnp.bfloat16)

    to_right = send(
        padded.at[:, pl.ds(ROWS, MARGIN)],
        padded.at[:, pl.ds(0, MARGIN)],
        halo_sem.at[0],
        halo_sem.at[1],
        right,
    )
    to_left = send(
        padded.at[:, pl.ds(MARGIN, MARGIN)],
        padded.at[:, pl.ds(ROWS + MARGIN, MARGIN)],
        halo_sem.at[2],
        halo_sem.at[3],
        left,
    )
    to_right.start()
    to_left.start()
    for load in loads[7:]:
        load.wait()
    to_right.wait()
    to_left.wait()
    wide[...] = padded[...].astype(jnp.float32)

    taps = taps_ref.shape[0]
    reach = MARGIN - taps // 2

    def act_copy(chunk):
        here = act.at[group, chunk]
        return send(here, here, act_send.at[chunk], act_recv.at[chunk], partner)

    chunks = half // 128
    for chunk in range(chunks):
        cols = slice(chunk * 128, (chunk + 1) * 128)
        far_cols = pl.ds(pl.multiple_of(offset + chunk * 128, 128), 128)
        weights = taps_ref[:, far_cols]
        filtered = []
        for which in range(2):
            total = jnp.zeros((ROWS, 128), jnp.float32)
            for phase in range(8):
                partial = None
                for tap in range(phase, taps, 8):
                    start = tap - phase
                    term = weights[tap : tap + 1] * wide[which, start : start + ROWS + 8, cols]
                    partial = term if partial is None else partial + term
                total = total + partial[phase + reach : phase + reach + ROWS]
            filtered.append(total)
        preact = filtered[0] + bias_ref[:, far_cols]
        gating = 1.0 / (1.0 + jnp.exp(-preact))
        act[group, chunk, 0] = (preact * gating).astype(jnp.bfloat16)
        act[group, chunk, 1] = (
            gating * (1.0 + preact * (1.0 - gating)) * filtered[1]
        ).astype(jnp.bfloat16)
        act_copy(chunk).start()

    def mix(source):
        rows = jnp.concatenate(
            [act[source, chunk].reshape(2 * ROWS, 128) for chunk in range(chunks)], axis=1
        )
        weight = wm_ref[pl.ds(pl.multiple_of(source * half, 128), half), :]
        return jnp.dot(rows, weight, preferred_element_type=jnp.float32)

    total = mix(group)
    for chunk in range(chunks):
        act_copy(chunk).wait()
    total = total + mix(1 - group)
    out_ref[...] = (wide[0, MARGIN : MARGIN + ROWS] + total[:ROWS]).astype(jnp.bfloat16)
    slope_ref[...] = (wide[1, MARGIN : MARGIN + ROWS] + total[ROWS:]).astype(jnp.bfloat16)

    for j in range(own):
        drain(kv.at[j, pl.ds(0, 2 * ys * (xs - 1) + ys)], kv_send.at[j])
        if zs > 1:
            drain(qq.at[j, pl.ds(0, ys * (zs - 1))], q_send.at[j])
            drain(part_out.at[j, pl.ds(0, zs - 1)], part_send.at[j])
        drain(joined.at[0, 0, pl.ds(0, 3)], head_send.at[j])


def shards(
    sizes,
    frames,
    tangent,
    norm_gain,
    query_weight,
    key_weight,
    value_weight,
    out_weight,
    conv_weight,
    conv_bias,
    mix_weight,
):
    zs, xs, ys, cs = sizes
    half = query_weight.shape[1]
    heads = half // HDIM
    own = heads // ys
    nk = xs * cs * ys
    sem = pltpu.SemaphoreType.DMA
    hbm = pl.BlockSpec(memory_space=pl.ANY)
    vmem = pl.BlockSpec(memory_space=pltpu.VMEM)
    shape = jax.ShapeDtypeStruct((ROWS, half), jnp.bfloat16)
    operands = (
        frames,
        tangent,
        norm_gain.reshape(1, -1),
        query_weight,
        key_weight,
        value_weight,
        out_weight,
        conv_weight,
        conv_bias.reshape(1, -1),
        mix_weight,
    )
    part = (own, zs, 2 * HDIM + STAT, ys * ROWS)
    return pl.pallas_call(
        functools.partial(kernel, sizes, heads),
        out_shape=(shape, shape),
        in_specs=[hbm] * len(operands),
        out_specs=(vmem, vmem),
        scratch_shapes=[pltpu.VMEM(value.shape, value.dtype) for value in operands]
        + [
            pltpu.VMEM((ys, own, 2, ROWS, 2 * HDIM), jnp.bfloat16),
            pltpu.VMEM((ys, own, 2 * HDIM, ROWS), jnp.bfloat16),
            pltpu.VMEM((own, nk, 2, ROWS, 2 * HDIM), jnp.bfloat16),
            pltpu.VMEM((own, zs * ys, 2 * HDIM, ROWS), jnp.bfloat16),
            pltpu.VMEM(part, jnp.bfloat16),
            pltpu.VMEM(part, jnp.bfloat16),
            pltpu.VMEM((own, ys, 2 * HDIM, ROWS), jnp.bfloat16),
            pltpu.VMEM((2, ys, own, 2 * HDIM, ROWS), jnp.bfloat16),
            pltpu.VMEM((half, half), jnp.bfloat16),
            pltpu.VMEM((2, ROWS + 2 * MARGIN, half), jnp.bfloat16),
            pltpu.VMEM((2, ROWS + 2 * MARGIN, half), jnp.float32),
            pltpu.VMEM((2, half // 128, 2, ROWS, 128), jnp.bfloat16),
            sem((len(operands),)),
            sem((2, own)),
            sem((2, own)),
            sem((own,)),
            sem((own, xs, ys)),
            sem((own, xs)),
            sem((own,)),
            sem((own,)),
            sem((own,)),
            sem((own,)),
            sem((own,)),
            sem((own,)),
            sem((2,)),
            sem((4,)),
            sem((half // 128,)),
            sem((half // 128,)),
        ],
        compiler_params=pltpu.CompilerParams(
            collective_id=0, has_side_effects=True, vmem_limit_bytes=48 * 1024 * 1024
        ),
        name="block",
    )(*operands)


def solution(mesh):
    sizes = FACTORS[mesh.shape["ctx"]]
    placed = (
        P("ctx", None),
        P("ctx", None),
        P(),
        P(None, "head"),
        P(None, "head"),
        P(None, "head"),
        P("head", None),
        P(),
        P(),
        P(None, "head"),
    )
    return jax.shard_map(
        functools.partial(shards, sizes),
        mesh=mesh,
        in_specs=placed,
        out_specs=(P("ctx", "head"), P("ctx", "head")),
        check_vma=False,
    )
```

time: 80.5 us -> 72.1 us (0.90)
  Pallas kernels: 69.4 us -> 60.2 us
    pallas_call x1, Pallas kernels: 69.4 us -> 60.2 us  [shards(): pl.pallas_call(functools.partial(kernel, sizes, heads), out_shape=(shape,...]
where the time goes in v2:
time: 72.1 us; the launch traced here: 70.9 us
  Pallas kernels  60.2 us (83%)
  local copies, waits for them, and re-layouts  10 us (14%)
    pallas_call x1, Pallas kernels, shards(): pl.pallas_call(functools.partial(kernel, sizes, heads), out_shape=(shape,...  60.2 us
    unnamed x20, local copies, waits for them, and re-layouts  9.35 us

profile of v2, /device:TPU:1, one launch (start us, length us, event | category | flops | bytes accessed | tf_op | source)
XLA Modules:
  0.0 70.9 jit_solution(6664288463208515421)
XLA Ops:
  0.6 0.0 copy-start.8
  0.6 0.7 reshape.10.gain_hbm
  1.3 0.0 copy-done.8
  1.3 0.0 copy-start
  1.4 1.1 %copy-done = bf16[768,384]{1,0:T(8,128)(2,1)S(1)} copy-done((bf16[768,384]{1,0:T(8,128)(2,1)S(1)}, bf16[768,384]{1,0:T(8,128)(2,1)}, u32[]{:S(2)}) %copy-start) | copy-done | bytes 589848
  2.4 0.0 copy-start.1
  2.4 1.1 %copy-done.1 = bf16[768,384]{1,0:T(8,128)(2,1)S(1)} copy-done((bf16[768,384]{1,0:T(8,128)(2,1)S(1)}, bf16[768,384]{1,0:T(8,128)(2,1)}, u32[]{:S(2)}) %copy-start.1) | copy-done | bytes 589848
  3.5 0.0 copy-start.2
  3.5 1.1 %copy-done.2 = bf16[768,384]{1,0:T(8,128)(2,1)S(1)} copy-done((bf16[768,384]{1,0:T(8,128)(2,1)S(1)}, bf16[768,384]{1,0:T(8,128)(2,1)}, u32[]{:S(2)}) %copy-start.2) | copy-done | bytes 589848
  4.5 0.0 copy-start.3
  4.5 1.1 %copy-done.3 = bf16[384,768]{1,0:T(8,128)(2,1)S(1)} copy-done((bf16[384,768]{1,0:T(8,128)(2,1)S(1)}, bf16[384,768]{1,0:T(8,128)(2,1)}, u32[]{:S(2)}) %copy-start.3) | copy-done | bytes 589848
  5.6 0.0 copy-start.4
  5.6 1.1 %copy-done.4 = bf16[768,384]{1,0:T(8,128)(2,1)S(1)} copy-done((bf16[768,384]{1,0:T(8,128)(2,1)S(1)}, bf16[768,384]{1,0:T(8,128)(2,1)}, u32[]{:S(2)}) %copy-start.4) | copy-done | bytes 589848
  6.7 0.0 copy-start.5
  6.7 0.9 %copy-done.5 = bf16[128,768]{1,0:T(8,128)(2,1)S(1)} copy-done((bf16[128,768]{1,0:T(8,128)(2,1)S(1)}, bf16[128,768]{1,0:T(8,128)(2,1)}, u32[]{:S(2)}) %copy-start.5) | copy-done | bytes 196632
  7.6 0.0 copy-start.6
  7.6 0.9 %copy-done.6 = bf16[128,768]{1,0:T(8,128)(2,1)S(1)} copy-done((bf16[128,768]{1,0:T(8,128)(2,1)S(1)}, bf16[128,768]{1,0:T(8,128)(2,1)}, u32[]{:S(2)}) %copy-start.6) | copy-done | bytes 196632
  8.5 0.0 copy-start.7
  8.5 0.9 %copy-done.7 = f32[31,768]{1,0:T(8,128)S(1)} copy-done((f32[31,768]{1,0:T(8,128)S(1)}, f32[31,768]{1,0:T(8,128)}, u32[]{:S(2)}) %copy-start.7) | copy-done | bytes 95256
  9.4 60.2 %block.1 = (bf16[128,384]{1,0:T(8,128)(2,1)S(1)}, bf16[128,384]{1,0:T(8,128)(2,1)S(1)}) custom-call(bf16[128,768]{1,0:T(8,128)(2,1)S(1)} %copy-done.5, bf16[128,768]{1,0:T(8,128)(2,1)S(1)} %copy-done.6, f32[1,768]{1,0:T(1,128)S(1)} %reshape.10.gain_hbm, bf16[768,384]{1,0:T(8,128)(2,1)S(1)} %copy-done, bf16[768,384]{1,0:T(8,128)(2,1)S(1)} %copy-done.1, ...), custom_call_target="tpu_custom_call" | custom-call | tf_op jit(solution)/shard_map/block/pallas_call | solution.py:497
  69.6 0.6 copy.14
  70.3 0.6 copy.15
  (1 shorter events, 0.0 us)
Async XLA Ops:
  0.6 0.7 copy-start.8
  1.3 1.1 %copy-start = (bf16[768,384]{1,0:T(8,128)(2,1)S(1)}, bf16[768,384]{1,0:T(8,128)(2,1)}, u32[]{:S(2)}) copy-start(bf16[768,384]{1,0:T(8,128)(2,1)} %wq_hbm.1) | copy-start | bytes 1769476
  2.4 1.1 %copy-start.1 = (bf16[768,384]{1,0:T(8,128)(2,1)S(1)}, bf16[768,384]{1,0:T(8,128)(2,1)}, u32[]{:S(2)}) copy-start(bf16[768,384]{1,0:T(8,128)(2,1)} %wk_hbm.1) | copy-start | bytes 1769476
  3.5 1.1 %copy-start.2 = (bf16[768,384]{1,0:T(8,128)(2,1)S(1)}, bf16[768,384]{1,0:T(8,128)(2,1)}, u32[]{:S(2)}) copy-start(bf16[768,384]{1,0:T(8,128)(2,1)} %wv_hbm.1) | copy-start | bytes 1769476
  4.5 1.1 %copy-start.3 = (bf16[384,768]{1,0:T(8,128)(2,1)S(1)}, bf16[384,768]{1,0:T(8,128)(2,1)}, u32[]{:S(2)}) copy-start(bf16[384,768]{1,0:T(8,128)(2,1)} %wo_hbm.1) | copy-start | bytes 1769476
  5.6 1.1 %copy-start.4 = (bf16[768,384]{1,0:T(8,128)(2,1)S(1)}, bf16[768,384]{1,0:T(8,128)(2,1)}, u32[]{:S(2)}) copy-start(bf16[768,384]{1,0:T(8,128)(2,1)} %wm_hbm.1) | copy-start | bytes 1769476
  6.7 0.9 %copy-start.5 = (bf16[128,768]{1,0:T(8,128)(2,1)S(1)}, bf16[128,768]{1,0:T(8,128)(2,1)}, u32[]{:S(2)}) copy-start(bf16[128,768]{1,0:T(8,128)(2,1)} %frames_hbm.1) | copy-start | bytes 589828
  7.6 0.9 %copy-start.6 = (bf16[128,768]{1,0:T(8,128)(2,1)S(1)}, bf16[128,768]{1,0:T(8,128)(2,1)}, u32[]{:S(2)}) copy-start(bf16[128,768]{1,0:T(8,128)(2,1)} %tangent_hbm.1) | copy-start | bytes 589828
  8.5 0.9 %copy-start.7 = (f32[31,768]{1,0:T(8,128)S(1)}, f32[31,768]{1,0:T(8,128)}, u32[]{:S(2)}) copy-start(f32[31,768]{1,0:T(8,128)} %taps_hbm.1) | copy-start | bytes 285700

commit v3 on v2

--- a/solution.py
+++ b/solution.py
@@ -39,13 +39,12 @@
     wm_hbm,
     out_ref,
     slope_ref,
-    frames_ref,
-    tangent_ref,
+    inputs,
     gain_ref,
     wq_ref,
     wk_ref,
     wv_ref,
-    wo_ref,
+    wo_all,
     taps_ref,
     bias_ref,
     wm_ref,
@@ -57,8 +56,6 @@
     part_in,
     merged,
     joined,
-    wo_far,
-    padded,
     wide,
     act,
     load_sem,
@@ -75,8 +72,6 @@
     head_recv,
     wo_sem,
     halo_sem,
-    act_send,
-    act_recv,
 ):
     zs, xs, ys, cs = sizes
     count = zs * xs * ys * cs
@@ -98,8 +93,14 @@
     fellow = (ctx_of(z, x, 1 - yl, core), group)
     partner = (me, 1 - group)
     diagonal = (ctx_of(z, x, 1 - yl, core), 1 - group)
-    right = (lax.rem(me + 1, count), group)
-    left = (lax.rem(me + count - 1, count), group)
+
+    def after(ctx):
+        return lax.rem(ctx + 1, count)
+
+    def before(ctx):
+        return lax.rem(ctx + count - 1, count)
+
+    right, left = (after(me), group), (before(me), group)
     x_peers = []
     for step in range(1, xs):
         other = lax.rem(x + step, xs)
@@ -112,14 +113,15 @@
     z_peers = [z_peer(step) for step in range(1, zs)]
 
     loads = []
+    body = pl.ds(MARGIN, ROWS)
     for source, target in (
-        (frames_hbm, frames_ref),
-        (tangent_hbm, tangent_ref),
+        (frames_hbm, inputs.at[0, body]),
+        (tangent_hbm, inputs.at[1, body]),
         (gain_hbm, gain_ref),
         (wk_hbm, wk_ref),
         (wv_hbm, wv_ref),
         (wq_hbm, wq_ref),
-        (wo_hbm, wo_ref),
+        (wo_hbm, wo_all.at[group]),
         (wm_hbm, wm_ref),
         (taps_hbm, taps_ref),
         (bias_hbm, bias_ref),
@@ -129,7 +131,13 @@
         loads.append(load)
 
     barrier = pltpu.get_barrier_semaphore()
-    everyone = [sibling, fellow, partner, diagonal, right, left]
+    everyone = []
+    near_square = lax.rem(z * xs + x + zs * xs + 2 * core - 1, zs * xs)
+    for g in (group, 1 - group):
+        for y in (yl, 1 - yl):
+            everyone += [(ctx_of(z, x, y, core), g), (ctx_of(z, x, y, 1 - core), g)]
+            everyone.append(((near_square * ys + y) * cs + 1 - core, g))
+    everyone = everyone[1:]
     everyone += [peer for _, peer in x_peers] + [peer for _, peer in z_peers]
     for peer in everyone:
         pl.semaphore_signal(barrier, inc=1, device_id=peer, device_id_type=MESH)
@@ -149,8 +157,8 @@
 
     for load in loads[:3]:
         load.wait()
-    plain = frames_ref[...].astype(jnp.float32)
-    slope = tangent_ref[...].astype(jnp.float32)
+    plain = inputs[0, body].astype(jnp.float32)
+    slope = inputs[1, body].astype(jnp.float32)
     gain = gain_ref[...]
     inverse = lax.rsqrt(jnp.mean(plain * plain, axis=-1, keepdims=True) + EPSILON)
     cross = jnp.mean(plain * slope, axis=-1, keepdims=True)
@@ -250,14 +258,25 @@
     relay(0)
     relay(1)
     loads[6].wait()
-    wo_copy = send(
-        wo_ref.at[:, pl.ds(pl.multiple_of((1 - group) * half, 128), half)],
-        wo_far,
-        wo_sem.at[0],
-        wo_sem.at[1],
-        partner,
+    here = wo_all.at[group]
+    wo_copy = send(here, here, wo_sem.at[0], wo_sem.at[1], partner)
+    wo_copy.start()
+    to_right = send(
+        inputs.at[:, pl.ds(ROWS, MARGIN)],
+        inputs.at[:, pl.ds(0, MARGIN)],
+        halo_sem.at[0],
+        halo_sem.at[1],
+        right,
     )
-    wo_copy.start()
+    to_left = send(
+        inputs.at[:, pl.ds(MARGIN, MARGIN)],
+        inputs.at[:, pl.ds(ROWS + MARGIN, MARGIN)],
+        halo_sem.at[2],
+        halo_sem.at[3],
+        left,
+    )
+    to_right.start()
+    to_left.start()
     forward(0)
     for j in range(2, own):
         relay(j)
@@ -318,13 +337,29 @@
             attended = attended + piece
             tilted = tilted + part_in[j, b, HDIM : 2 * HDIM].astype(jnp.float32) * shares[b]
             tilted = tilted + piece * (centers[b] - middle)
-        result = jnp.concatenate([attended, tilted], axis=0).astype(jnp.bfloat16)
+        result = jnp.concatenate([attended, tilted], axis=0)
         for y in range(ys):
-            merged[j, y] = result[:, y * ROWS : (y + 1) * ROWS]
-        here = joined.at[group, yl, j]
-        for peer, row_block in ((fellow, 1 - yl), (diagonal, 1 - yl), (partner, yl)):
-            send(merged.at[j, row_block], here, head_send.at[j], head_recv.at[j], peer).start()
-        joined[group, yl, j] = merged[j, yl]
+            merged[j, y] = result[:, y * ROWS : (y + 1) * ROWS].T.astype(jnp.bfloat16)
+        joined[group, yl, j, body] = merged[j, yl]
+
+        def hand(source, target, peer):
+            send(source, target, head_send.at[j], head_recv.at[j], peer).start()
+
+        for peer, block in ((fellow, 1 - yl), (diagonal, 1 - yl), (partner, yl)):
+            hand(merged.at[j, block], joined.at[group, yl, j, body], peer)
+        for y in range(ys):
+            ctx = ctx_of(z, x, y, core)
+            for g in (group, 1 - group):
+                hand(
+                    merged.at[j, y, pl.ds(0, MARGIN)],
+                    joined.at[group, yl, j, pl.ds(MARGIN + ROWS, MARGIN)],
+                    (before(ctx), g),
+                )
+                hand(
+                    merged.at[j, y, pl.ds(ROWS - MARGIN, MARGIN)],
+                    joined.at[group, yl, j, pl.ds(0, MARGIN)],
+                    (after(ctx), g),
+                )
 
     @pl.loop(0, own)
     def _(j):
@@ -361,63 +396,43 @@
 
     combine(own - 1)
 
+    low = lax.broadcasted_iota(jnp.int32, (ROWS + 2 * MARGIN, 2 * HDIM), 1) < HDIM
+
+    def project_out(j):
+        drain(merged.at[pl.ds(0, 2)], head_recv.at[j])
+        outs, slopes, weights = [], [], []
+        for g in range(2):
+            first = joined[g, 0, j].astype(jnp.float32)
+            second = joined[g, 1, j].astype(jnp.float32)
+            outs.append(jnp.where(low, first, pltpu.roll(second, HDIM, 1)))
+            slopes.append(jnp.where(low, pltpu.roll(first, HDIM, 1), second))
+            for y in range(ys):
+                weights.append(wo_all[g, pl.ds((y * own + j) * HDIM, HDIM)])
+        rows = jnp.concatenate(
+            [jnp.concatenate(outs, axis=1), jnp.concatenate(slopes, axis=1)], axis=0
+        )
+        return jnp.dot(
+            rows.astype(jnp.bfloat16),
+            jnp.concatenate(weights, axis=0),
+            preferred_element_type=jnp.float32,
+        )
+
     wo_copy.wait()
-    for j in range(own):
-        drain(joined.at[0, 0, pl.ds(0, 3)], head_recv.at[j])
-
-    offset = pl.multiple_of(group * half, 128)
-    own_cols = pl.ds(offset, half)
-
-    def rows_of(source, lower):
-        stacked = joined[source, :, :, lower : lower + HDIM].reshape(half, ROWS)
-        return stacked.astype(jnp.float32).T.astype(jnp.bfloat16)
-
-    def heads_of(source):
-        return jnp.concatenate([rows_of(source, 0), rows_of(source, HDIM)], axis=0)
-
-    mixing = jnp.dot(heads_of(group), wo_ref[:, own_cols], preferred_element_type=jnp.float32)
-    mixing += jnp.dot(heads_of(1 - group), wo_far[...], preferred_element_type=jnp.float32)
-    padded[0, MARGIN : MARGIN + ROWS] = (
-        frames_ref[:, own_cols].astype(jnp.float32) + mixing[:ROWS]
-    ).astype(jnp.bfloat16)
-    padded[1, MARGIN : MARGIN + ROWS] = (
-        tangent_ref[:, own_cols].astype(jnp.float32) + mixing[ROWS:]
-    ).astype(jnp.bfloat16)
-
-    to_right = send(
-        padded.at[:, pl.ds(ROWS, MARGIN)],
-        padded.at[:, pl.ds(0, MARGIN)],
-        halo_sem.at[0],
-        halo_sem.at[1],
-        right,
-    )
-    to_left = send(
-        padded.at[:, pl.ds(MARGIN, MARGIN)],
-        padded.at[:, pl.ds(ROWS + MARGIN, MARGIN)],
-        halo_sem.at[2],
-        halo_sem.at[3],
-        left,
-    )
-    to_right.start()
-    to_left.start()
+    to_right.wait()
+    to_left.wait()
+    mixing = functools.reduce(jnp.add, [project_out(j) for j in range(own)])
+    length = ROWS + 2 * MARGIN
+    for which in range(2):
+        mixed = inputs[which].astype(jnp.float32) + mixing[which * length : (which + 1) * length]
+        wide[which] = mixed.astype(jnp.bfloat16).astype(jnp.float32)
+
     for load in loads[7:]:
         load.wait()
-    to_right.wait()
-    to_left.wait()
-    wide[...] = padded[...].astype(jnp.float32)
-
     taps = taps_ref.shape[0]
     reach = MARGIN - taps // 2
-
-    def act_copy(chunk):
-        here = act.at[group, chunk]
-        return send(here, here, act_send.at[chunk], act_recv.at[chunk], partner)
-
-    chunks = half // 128
-    for chunk in range(chunks):
+    for chunk in range(wide.shape[2] // 128):
         cols = slice(chunk * 128, (chunk + 1) * 128)
-        far_cols = pl.ds(pl.multiple_of(offset + chunk * 128, 128), 128)
-        weights = taps_ref[:, far_cols]
+        weights = taps_ref[:, cols]
         filtered = []
         for which in range(2):
             total = jnp.zeros((ROWS, 128), jnp.float32)
@@ -429,34 +444,24 @@
                     partial = term if partial is None else partial + term
                 total = total + partial[phase + reach : phase + reach + ROWS]
             filtered.append(total)
-        preact = filtered[0] + bias_ref[:, far_cols]
+        preact = filtered[0] + bias_ref[:, cols]
         gating = 1.0 / (1.0 + jnp.exp(-preact))
-        act[group, chunk, 0] = (preact * gating).astype(jnp.bfloat16)
-        act[group, chunk, 1] = (
+        act[:ROWS, cols] = (preact * gating).astype(jnp.bfloat16)
+        act[ROWS:, cols] = (
             gating * (1.0 + preact * (1.0 - gating)) * filtered[1]
         ).astype(jnp.bfloat16)
-        act_copy(chunk).start()
-
-    def mix(source):
-        rows = jnp.concatenate(
-            [act[source, chunk].reshape(2 * ROWS, 128) for chunk in range(chunks)], axis=1
-        )
-        weight = wm_ref[pl.ds(pl.multiple_of(source * half, 128), half), :]
-        return jnp.dot(rows, weight, preferred_element_type=jnp.float32)
-
-    total = mix(group)
-    for chunk in range(chunks):
-        act_copy(chunk).wait()
-    total = total + mix(1 - group)
-    out_ref[...] = (wide[0, MARGIN : MARGIN + ROWS] + total[:ROWS]).astype(jnp.bfloat16)
-    slope_ref[...] = (wide[1, MARGIN : MARGIN + ROWS] + total[ROWS:]).astype(jnp.bfloat16)
+
+    total = jnp.dot(act[...], wm_ref[...], preferred_element_type=jnp.float32)
+    own_cols = pl.ds(pl.multiple_of(group * half, 128), half)
+    out_ref[...] = (wide[0, body, own_cols] + total[:ROWS]).astype(jnp.bfloat16)
+    slope_ref[...] = (wide[1, body, own_cols] + total[ROWS:]).astype(jnp.bfloat16)
 
     for j in range(own):
         drain(kv.at[j, pl.ds(0, 2 * ys * (xs - 1) + ys)], kv_send.at[j])
         if zs > 1:
             drain(qq.at[j, pl.ds(0, ys * (zs - 1))], q_send.at[j])
             drain(part_out.at[j, pl.ds(0, zs - 1)], part_send.at[j])
-        drain(joined.at[0, 0, pl.ds(0, 3)], head_send.at[j])
+        drain(merged.at[pl.ds(0, 2)], head_send.at[j])
 
 
 def shards(
@@ -473,10 +478,11 @@
     mix_weight,
 ):
     zs, xs, ys, cs = sizes
-    half = query_weight.shape[1]
+    width, half = query_weight.shape
     heads = half // HDIM
     own = heads // ys
     nk = xs * cs * ys
+    length = ROWS + 2 * MARGIN
     sem = pltpu.SemaphoreType.DMA
     hbm = pl.BlockSpec(memory_space=pl.ANY)
     vmem = pl.BlockSpec(memory_space=pltpu.VMEM)
@@ -499,20 +505,26 @@
         out_shape=(shape, shape),
         in_specs=[hbm] * len(operands),
         out_specs=(vmem, vmem),
-        scratch_shapes=[pltpu.VMEM(value.shape, value.dtype) for value in operands]
-        + [
+        scratch_shapes=[
+            pltpu.VMEM((2, length, width), jnp.bfloat16),
+            pltpu.VMEM((1, width), jnp.float32),
+            pltpu.VMEM((width, half), jnp.bfloat16),
+            pltpu.VMEM((width, half), jnp.bfloat16),
+            pltpu.VMEM((width, half), jnp.bfloat16),
+            pltpu.VMEM((2, half, width), jnp.bfloat16),
+            pltpu.VMEM(conv_weight.shape, jnp.float32),
+            pltpu.VMEM((1, width), jnp.float32),
+            pltpu.VMEM((width, half), jnp.bfloat16),
             pltpu.VMEM((ys, own, 2, ROWS, 2 * HDIM), jnp.bfloat16),
             pltpu.VMEM((ys, own, 2 * HDIM, ROWS), jnp.bfloat16),
             pltpu.VMEM((own, nk, 2, ROWS, 2 * HDIM), jnp.bfloat16),
             pltpu.VMEM((own, zs * ys, 2 * HDIM, ROWS), jnp.bfloat16),
             pltpu.VMEM(part, jnp.bfloat16),
             pltpu.VMEM(part, jnp.bfloat16),
-            pltpu.VMEM((own, ys, 2 * HDIM, ROWS), jnp.bfloat16),
-            pltpu.VMEM((2, ys, own, 2 * HDIM, ROWS), jnp.bfloat16),
-            pltpu.VMEM((half, half), jnp.bfloat16),
-            pltpu.VMEM((2, ROWS + 2 * MARGIN, half), jnp.bfloat16),
-            pltpu.VMEM((2, ROWS + 2 * MARGIN, half), jnp.float32),
-            pltpu.VMEM((2, half // 128, 2, ROWS, 128), jnp.bfloat16),
+            pltpu.VMEM((own, ys, ROWS, 2 * HDIM), jnp.bfloat16),
+            pltpu.VMEM((2, ys, own, length, 2 * HDIM), jnp.bfloat16),
+            pltpu.VMEM((2, length, width), jnp.float32),
+            pltpu.VMEM((2 * ROWS, width), jnp.bfloat16),
             sem((len(operands),)),
             sem((2, own)),
             sem((2, own)),
@@ -527,11 +539,9 @@
             sem((own,)),
             sem((2,)),
             sem((4,)),
-            sem((half // 128,)),
-            sem((half // 128,)),
         ],
         compiler_params=pltpu.CompilerParams(
-            collective_id=0, has_side_effects=True, vmem_limit_bytes=48 * 1024 * 1024
+            collective_id=0, has_side_effects=True, vmem_limit_bytes=60 * 1024 * 1024
         ),
         name="block",
     )(*operands)

time: 72.1 us -> 59.6 us (0.83); the launches traced: 70.9 us -> 59.4 us
  local copies, waits for them, and re-layouts: 10 us -> 4.08 us
  Pallas kernels: 60.2 us -> 54.7 us
    unnamed x20 -> x6, local copies, waits for them, and re-layouts: 9.35 us -> 2.23 us
    pallas_call x1, Pallas kernels: 60.2 us -> 54.7 us  [shards(): pl.pallas_call(functools.partial(kernel, sizes, heads), out_shape=(shape,...]
where the time goes in v3:
time: 59.6 us; the launch traced here: 59.4 us
  Pallas kernels  54.7 us (92%)
  local copies, waits for them, and re-layouts  4.08 us (7%)
  between operations  0.66 us (1%)
    pallas_call x1, Pallas kernels, shards(): pl.pallas_call(functools.partial(kernel, sizes, heads), out_shape=(shape,...  54.7 us
    unnamed x6, local copies, waits for them, and re-layouts  2.23 us
    reshape x1, local copies, waits for them, and re-layouts, shards(): norm_gain.reshape(1, -1)  1.27 us

profile of v3, /device:TPU:1, one launch (start us, length us, event | category | flops | bytes accessed | tf_op | source)
XLA Modules:
  0.0 59.4 jit_solution(8939338022097691473)
XLA Ops:
  0.6 0.0 copy-start.1
  0.6 1.3 %reshape.10.gain_hbm = f32[1,768]{1,0:T(1,128)} reshape(f32[768]{0:T(1024)} %param.12) | data formatting | bytes 6144 | tf_op jit(solution)/shard_map/reshape | solution.py:493
  1.9 0.0 copy-done.1
  1.9 0.6 reshape.11.bias_hbm
  2.5 54.7 %block.1 = (bf16[128,384]{1,0:T(8,128)(2,1)}, bf16[128,384]{1,0:T(8,128)(2,1)}) custom-call(bf16[128,768]{1,0:T(8,128)(2,1)} %frames_hbm.1, bf16[128,768]{1,0:T(8,128)(2,1)} %tangent_hbm.1, f32[1,768]{1,0:T(1,128)} %reshape.10.gain_hbm, bf16[768,384]{1,0:T(8,128)(2,1)} %wq_hbm.1, bf16[768,384]{1,0:T(8,128)(2,1)} %wk_hbm.1, bf16[768,384]{1,0:T(8,128)(2,1)} %wv_hbm.1, ...), custom_call_target="tpu_custom_call" | custom-call | tf_op jit(solution)/shard_map/block/pallas_call | solution.py:503
  57.2 0.0 copy-start
  57.2 1.6 %copy.14 = bf16[128,384]{1,0:T(8,128)(2,1)} copy(bf16[128,384]{1,0:T(8,128)(2,1)} %get-tuple-element.4) | data formatting | bytes 196608
  58.7 0.0 copy-done
  58.7 0.6 %copy.15 = bf16[128,384]{1,0:T(8,128)(2,1)} copy(bf16[128,384]{1,0:T(8,128)(2,1)S(1)} %copy-done) | data formatting | bytes 196608
Async XLA Ops:
  0.6 1.3 %copy-start.1 = (f32[768]{0:T(1024)S(1)}, f32[768]{0:T(1024)}, u32[]{:S(2)}) copy-start(f32[768]{0:T(1024)} %param.18) | copy-start | bytes 9220
  57.2 1.6 %copy-start = (bf16[128,384]{1,0:T(8,128)(2,1)S(1)}, bf16[128,384]{1,0:T(8,128)(2,1)}, u32[]{:S(2)}) copy-start(bf16[128,384]{1,0:T(8,128)(2,1)} %get-tuple-element.5) | copy-start | bytes 294916

commit v4 on v3

--- a/solution.py
+++ b/solution.py
@@ -58,6 +58,11 @@
     joined,
     wide,
     act,
+    product_even,
+    product_odd,
+    chances,
+    peak_even,
+    peak_odd,
     load_sem,
     relay_sem,
     relay_q_sem,
@@ -102,7 +107,7 @@
 
     right, left = (after(me), group), (before(me), group)
     x_peers = []
-    for step in range(1, xs):
+    for step in sorted(range(1, xs), key=lambda step: min(step, xs - step)):
         other = lax.rem(x + step, xs)
         x_peers.append((other, (ctx_of(z, other, yl, core), group)))
 
@@ -159,7 +164,7 @@
         load.wait()
     plain = inputs[0, body].astype(jnp.float32)
     slope = inputs[1, body].astype(jnp.float32)
-    gain = gain_ref[...]
+    gain = gain_ref[...].reshape(1, -1)
     inverse = lax.rsqrt(jnp.mean(plain * plain, axis=-1, keepdims=True) + EPSILON)
     cross = jnp.mean(plain * slope, axis=-1, keepdims=True)
     normed = (plain * inverse * gain).astype(jnp.bfloat16)
@@ -231,23 +236,33 @@
         here = kv.at[j, pl.ds(slot(source, core, 0), ys)]
         return send(here, here, kv_send.at[j], sibling_recv.at[j, source], sibling)
 
-    for j in range(own):
+    def spread(j, which):
+        for _, peer in x_peers:
+            direct(j, which, peer).start()
+
+    def hand_over(j):
         relay_kv(j).start()
         relay_q(j).start()
+
+    hand_over(0)
+    for j in range(own):
         kv[j, slot(x, core, yl)] = stage_kv[yl, j]
         qq[j, z * ys + yl] = stage_q[yl, j]
-        for _, peer in x_peers:
-            direct(j, yl, peer).start()
+        if j == 0:
+            spread(0, yl)
+            for other in range(1, own):
+                hand_over(other)
 
     def relay(j):
         relay_kv(j).wait()
-        for _, peer in x_peers:
-            direct(j, 1 - yl, peer).start()
+        spread(j, 1 - yl)
         pass_on(j, x).start()
         relay_q(j).wait()
         here = qq.at[j, pl.ds(z * ys, ys)]
         for _, peer in z_peers:
-            send(here, here, q_send.at[j], q_recv.at[j], peer).start()
+            send(here, here, q_send.at[j], q_recv.at[j, z], peer).start()
+        if j < own - 1:
+            spread(j + 1, yl)
 
     def forward(j):
         for other, _ in x_peers:
@@ -255,8 +270,9 @@
                 drain(kv.at[j, slot(other, core, which)], direct_recv.at[j, other, which])
             pass_on(j, other).start()
 
-    relay(0)
-    relay(1)
+    for j in range(own):
+        relay(j)
+    forward(0)
     loads[6].wait()
     here = wo_all.at[group]
     wo_copy = send(here, here, wo_sem.at[0], wo_sem.at[1], partner)
@@ -277,31 +293,72 @@
     )
     to_right.start()
     to_left.start()
-    forward(0)
-    for j in range(2, own):
-        relay(j)
-
-    def attend(j, other):
-        key_rows = kv[j, :, 0].reshape(nk * ROWS, 2 * HDIM)
-        value_cols = jnp.concatenate([kv[j, b, 1] for b in range(nk)], axis=1)
+
+    tiles = own * zs
+    chunk_rows = min(512, nk * ROWS)
+    chunk_blocks = chunk_rows // ROWS
+    step_rows = 64
+
+    away = own * (zs - 1)
+
+    def tile_of(u):
+        if zs == 1:
+            return u, 0
+        early = u < away
+        j = jnp.where(early, u // (zs - 1), u - away)
+        return j, jnp.where(early, lax.rem(u, zs - 1), zs - 1)
+
+    def queries_of(u):
+        j, tile = tile_of(u)
+        other, _ = z_peer(tile + 1)
         blocks = [qq[j, other * ys + y] for y in range(ys)]
         plain_q = jnp.concatenate([block[:HDIM] for block in blocks], axis=1)
         slope_q = jnp.concatenate([block[HDIM:] for block in blocks], axis=1)
         top = jnp.concatenate([plain_q, slope_q], axis=1)
         bottom = jnp.concatenate([jnp.zeros_like(plain_q), plain_q], axis=1)
-        product = jnp.dot(
-            key_rows, jnp.concatenate([top, bottom], axis=0), preferred_element_type=jnp.float32
-        )
-        scores, slopes = product[:, :span], product[:, span:]
-        peak = jnp.max(scores, axis=0, keepdims=True)
-        weights = jnp.exp(scores - peak)
-        slanted = weights * slopes
-        totals = jnp.sum(weights, axis=0, keepdims=True)
-        moments = jnp.sum(slanted, axis=0, keepdims=True)
-        stacked = jnp.concatenate(
-            [weights.astype(jnp.bfloat16), slanted.astype(jnp.bfloat16)], axis=1
-        )
-        sums = jnp.dot(value_cols, stacked, preferred_element_type=jnp.float32)
+        return jnp.concatenate([top, bottom], axis=0)
+
+    def work(current, following, product_now, peak_now, product_next, peak_next):
+        if current is not None:
+            j, tile = tile_of(current)
+            peak = jnp.max(peak_now[...], axis=0, keepdims=True)
+            totals = jnp.zeros((8, span), jnp.float32)
+            moments = jnp.zeros((8, span), jnp.float32)
+            sums = None
+        if following is not None:
+            next_j, _ = tile_of(following)
+            next_queries = queries_of(following)
+            highest = jnp.full((8, span), -jnp.inf, jnp.float32)
+        for first in range(0, nk, chunk_blocks):
+            chunk = slice(first * ROWS, (first + chunk_blocks) * ROWS)
+            if current is not None:
+                for start in range(chunk.start, chunk.stop, step_rows):
+                    rows = slice(start, start + step_rows)
+                    weights = jnp.exp(product_now[rows, :span] - peak)
+                    slanted = weights * product_now[rows, span:]
+                    totals = totals + jnp.sum(weights.reshape(-1, 8, span), axis=0)
+                    moments = moments + jnp.sum(slanted.reshape(-1, 8, span), axis=0)
+                    chances[rows, :span] = weights.astype(jnp.bfloat16)
+                    chances[rows, span:] = slanted.astype(jnp.bfloat16)
+                value_cols = jnp.concatenate(
+                    [kv[j, first + b, 1] for b in range(chunk_blocks)], axis=1
+                )
+                part = jnp.dot(value_cols, chances[chunk], preferred_element_type=jnp.float32)
+                sums = part if sums is None else sums + part
+            if following is not None:
+                key_rows = kv[next_j, pl.ds(first, chunk_blocks), 0].reshape(chunk_rows, 2 * HDIM)
+                product = jnp.dot(key_rows, next_queries, preferred_element_type=jnp.float32)
+                product_next[chunk] = product
+                highest = jnp.maximum(
+                    highest, jnp.max(product[:, :span].reshape(-1, 8, span), axis=0)
+                )
+        if following is not None:
+            peak_next[...] = highest
+        if current is None:
+            return
+        other, peer = z_peer(tile + 1)
+        totals = jnp.sum(totals, axis=0, keepdims=True)
+        moments = jnp.sum(moments, axis=0, keepdims=True)
         share = 1.0 / totals
         center = moments * share
         attended = sums[:HDIM, :span] * share
@@ -315,6 +372,16 @@
         part_out[j, other, :HDIM] = attended.astype(jnp.bfloat16)
         part_out[j, other, HDIM : 2 * HDIM] = tilted.astype(jnp.bfloat16)
         part_out[j, other, 2 * HDIM :] = stats.astype(jnp.bfloat16)
+
+        @pl.when(tile < zs - 1)
+        def _():
+            send(
+                part_out.at[j, other],
+                part_in.at[j, z],
+                part_send.at[j],
+                part_recv.at[j],
+                peer,
+            ).start()
 
     def combine(j):
         part_in[j, z] = part_out[j, z]
@@ -361,39 +428,43 @@
                     (after(ctx), g),
                 )
 
-    @pl.loop(0, own)
-    def _(j):
-        for step in range(xs):
-            source = lax.rem(x + step, xs)
-            drain(
-                kv.at[j, pl.ds(slot(source, 1 - core, 0), ys)], sibling_recv.at[j, source]
-            )
-        if zs > 1:
-            drain(qq.at[j, pl.ds(0, ys * (zs - 1))], q_recv.at[j])
-
-        @pl.loop(0, zs)
-        def _(tile):
-            other, peer = z_peer(tile + 1)
-            attend(j, other)
-
-            @pl.when(tile < zs - 1)
-            def _():
-                send(
-                    part_out.at[j, other],
-                    part_in.at[j, z],
-                    part_send.at[j],
-                    part_recv.at[j],
-                    peer,
-                ).start()
-
-            @pl.when(jnp.logical_and(tile == 0, j < own - 1))
-            def _():
-                forward(j + 1)
-
-        @pl.when(j >= 1)
+    def prepare(u):
+        j, tile = tile_of(u)
+        other, _ = z_peer(tile + 1)
+
+        @pl.when(u < away)
         def _():
-            combine(j - 1)
-
+            drain(qq.at[j, pl.ds(other * ys, ys)], q_recv.at[j, other])
+
+        @pl.when(tile == 0)
+        def _():
+            for step in range(xs):
+                source = lax.rem(x + step, xs)
+                drain(kv.at[j, pl.ds(slot(source, 1 - core, 0), ys)], sibling_recv.at[j, source])
+
+        @pl.when(jnp.logical_and(tile == max(zs - 2, 0), j < own - 1))
+        def _():
+            forward(j + 1)
+
+    even, odd = (product_even, peak_even), (product_odd, peak_odd)
+
+    prepare(0)
+    work(None, 0, *odd, *even)
+
+    @pl.loop(0, tiles // 2 - 1)
+    def _(pair):
+        u = 2 * pair
+        prepare(u + 1)
+        work(u, u + 1, *even, *odd)
+        prepare(u + 2)
+        work(u + 1, u + 2, *odd, *even)
+
+    for j in range(own - 2):
+        combine(j)
+    prepare(tiles - 1)
+    work(tiles - 2, tiles - 1, *even, *odd)
+    combine(own - 2)
+    work(tiles - 1, None, *odd, *even)
     combine(own - 1)
 
     low = lax.broadcasted_iota(jnp.int32, (ROWS + 2 * MARGIN, 2 * HDIM), 1) < HDIM
@@ -444,7 +515,7 @@
                     partial = term if partial is None else partial + term
                 total = total + partial[phase + reach : phase + reach + ROWS]
             filtered.append(total)
-        preact = filtered[0] + bias_ref[:, cols]
+        preact = filtered[0] + bias_ref[cols].reshape(1, -1)
         gating = 1.0 / (1.0 + jnp.exp(-preact))
         act[:ROWS, cols] = (preact * gating).astype(jnp.bfloat16)
         act[ROWS:, cols] = (
@@ -490,13 +561,13 @@
     operands = (
         frames,
         tangent,
-        norm_gain.reshape(1, -1),
+        norm_gain,
         query_weight,
         key_weight,
         value_weight,
         out_weight,
         conv_weight,
-        conv_bias.reshape(1, -1),
+        conv_bias,
         mix_weight,
     )
     part = (own, zs, 2 * HDIM + STAT, ys * ROWS)
@@ -507,13 +578,13 @@
         out_specs=(vmem, vmem),
         scratch_shapes=[
             pltpu.VMEM((2, length, width), jnp.bfloat16),
-            pltpu.VMEM((1, width), jnp.float32),
+            pltpu.VMEM((width,), jnp.float32),
             pltpu.VMEM((width, half), jnp.bfloat16),
             pltpu.VMEM((width, half), jnp.bfloat16),
             pltpu.VMEM((width, half), jnp.bfloat16),
             pltpu.VMEM((2, half, width), jnp.bfloat16),
             pltpu.VMEM(conv_weight.shape, jnp.float32),
-            pltpu.VMEM((1, width), jnp.float32),
+            pltpu.VMEM((width,), jnp.float32),
             pltpu.VMEM((width, half), jnp.bfloat16),
             pltpu.VMEM((ys, own, 2, ROWS, 2 * HDIM), jnp.bfloat16),
             pltpu.VMEM((ys, own, 2 * HDIM, ROWS), jnp.bfloat16),
@@ -525,6 +596,11 @@
             pltpu.VMEM((2, ys, own, length, 2 * HDIM), jnp.bfloat16),
             pltpu.VMEM((2, length, width), jnp.float32),
             pltpu.VMEM((2 * ROWS, width), jnp.bfloat16),
+            pltpu.VMEM((nk * ROWS, 2 * ys * ROWS), jnp.float32),
+            pltpu.VMEM((nk * ROWS, 2 * ys * ROWS), jnp.float32),
+            pltpu.VMEM((nk * ROWS, 2 * ys * ROWS), jnp.bfloat16),
+            pltpu.VMEM((8, ys * ROWS), jnp.float32),
+            pltpu.VMEM((8, ys * ROWS), jnp.float32),
             sem((len(operands),)),
             sem((2, own)),
             sem((2, own)),
@@ -532,7 +608,7 @@
             sem((own, xs, ys)),
             sem((own, xs)),
             sem((own,)),
-            sem((own,)),
+            sem((own, zs)),
             sem((own,)),
             sem((own,)),
             sem((own,)),

time: 59.6 us -> 51.6 us (0.87)
  Pallas kernels: 54.7 us -> 48.6 us
  local copies, waits for them, and re-layouts: 4.08 us -> 2.22 us
    pallas_call x1, Pallas kernels: 54.7 us -> 48.6 us  [shards(): pl.pallas_call(functools.partial(kernel, sizes, heads), out_shape=(shape,...]
    reshape x2 -> x0, local copies, waits for them, and re-layouts: 1.85 us -> none  [the longest x1 1.27 us: shards(): norm_gain.reshape(1, -1)]
    unnamed x6 -> x4, local copies, waits for them, and re-layouts: 2.23 us -> 2.22 us
where the time goes in v4:
time: 51.6 us; the launch traced here: 51.5 us
  Pallas kernels  48.6 us (94%)
  local copies, waits for them, and re-layouts  2.22 us (4%)
  between operations  0.65 us (1%)
    pallas_call x1, Pallas kernels, shards(): pl.pallas_call(functools.partial(kernel, sizes, heads), out_shape=(shape,...  48.6 us
    unnamed x4, local copies, waits for them, and re-layouts  2.22 us

profile of v4, /device:TPU:1, one launch (start us, length us, event | category | flops | bytes accessed | tf_op | source)
XLA Modules:
  0.0 51.5 jit_solution(1948727739842101873)
XLA Ops:
  0.6 48.6 %block.1 = (bf16[128,384]{1,0:T(8,128)(2,1)}, bf16[128,384]{1,0:T(8,128)(2,1)}) custom-call(bf16[128,768]{1,0:T(8,128)(2,1)} %frames_hbm.1, bf16[128,768]{1,0:T(8,128)(2,1)} %tangent_hbm.1, f32[768]{0:T(1024)} %gain_hbm.1, bf16[768,384]{1,0:T(8,128)(2,1)} %wq_hbm.1, bf16[768,384]{1,0:T(8,128)(2,1)} %wk_hbm.1, bf16[768,384]{1,0:T(8,128)(2,1)} %wv_hbm.1, ...), custom_call_target="tpu_custom_call" | custom-call | tf_op jit(solution)/shard_map/block/pallas_call | solution.py:574
  49.2 0.0 copy-start
  49.2 1.6 %copy.14 = bf16[128,384]{1,0:T(8,128)(2,1)} copy(bf16[128,384]{1,0:T(8,128)(2,1)} %get-tuple-element.4) | data formatting | bytes 196608
  50.8 0.0 copy-done
  50.8 0.6 %copy.15 = bf16[128,384]{1,0:T(8,128)(2,1)} copy(bf16[128,384]{1,0:T(8,128)(2,1)S(1)} %copy-done) | data formatting | bytes 196608
Async XLA Ops:
  49.2 1.6 %copy-start = (bf16[128,384]{1,0:T(8,128)(2,1)S(1)}, bf16[128,384]{1,0:T(8,128)(2,1)}, u32[]{:S(2)}) copy-start(bf16[128,384]{1,0:T(8,128)(2,1)} %get-tuple-element.5) | copy-start | bytes 294916

commit v5 on v4

--- a/solution.py
+++ b/solution.py
@@ -38,7 +38,6 @@
     bias_hbm,
     wm_hbm,
     out_ref,
-    slope_ref,
     inputs,
     gain_ref,
     wq_ref,
@@ -195,15 +194,10 @@
 
     loads[4].wait()
     values, value_slope = turned(project(wv_ref))
-    loads[5].wait()
-    queries, query_slope = turned(project(wq_ref))
-    queries, query_slope = queries * 0.125, query_slope * 0.125
     for h in range(heads):
         rows = slice(h * HDIM, (h + 1) * HDIM)
         stage_kv[h // own, h % own, 1, :HDIM] = values[rows]
         stage_kv[h // own, h % own, 1, HDIM:] = value_slope[rows]
-        stage_q[h // own, h % own, :HDIM] = queries[rows]
-        stage_q[h // own, h % own, HDIM:] = query_slope[rows]
 
     pl.semaphore_wait(barrier, len(everyone))
 
@@ -240,18 +234,25 @@
         for _, peer in x_peers:
             direct(j, which, peer).start()
 
-    def hand_over(j):
+    for j in range(own):
         relay_kv(j).start()
+        if j == 0:
+            kv[0, slot(x, core, yl)] = stage_kv[yl, 0]
+            spread(0, yl)
+
+    loads[5].wait()
+    queries, query_slope = turned(project(wq_ref))
+    queries, query_slope = queries * 0.125, query_slope * 0.125
+    for h in range(heads):
+        rows = slice(h * HDIM, (h + 1) * HDIM)
+        stage_q[h // own, h % own, :HDIM] = queries[rows]
+        stage_q[h // own, h % own, HDIM:] = query_slope[rows]
+    for j in range(own):
         relay_q(j).start()
-
-    hand_over(0)
     for j in range(own):
-        kv[j, slot(x, core, yl)] = stage_kv[yl, j]
+        if j > 0:
+            kv[j, slot(x, core, yl)] = stage_kv[yl, j]
         qq[j, z * ys + yl] = stage_q[yl, j]
-        if j == 0:
-            spread(0, yl)
-            for other in range(1, own):
-                hand_over(other)
 
     def relay(j):
         relay_kv(j).wait()
@@ -412,8 +413,6 @@
         def hand(source, target, peer):
             send(source, target, head_send.at[j], head_recv.at[j], peer).start()
 
-        for peer, block in ((fellow, 1 - yl), (diagonal, 1 - yl), (partner, yl)):
-            hand(merged.at[j, block], joined.at[group, yl, j, body], peer)
         for y in range(ys):
             ctx = ctx_of(z, x, y, core)
             for g in (group, 1 - group):
@@ -427,6 +426,8 @@
                     joined.at[group, yl, j, pl.ds(0, MARGIN)],
                     (after(ctx), g),
                 )
+        for peer, block in ((fellow, 1 - yl), (diagonal, 1 - yl), (partner, yl)):
+            hand(merged.at[j, block], joined.at[group, yl, j, body], peer)
 
     def prepare(u):
         j, tile = tile_of(u)
@@ -524,8 +525,8 @@
 
     total = jnp.dot(act[...], wm_ref[...], preferred_element_type=jnp.float32)
     own_cols = pl.ds(pl.multiple_of(group * half, 128), half)
-    out_ref[...] = (wide[0, body, own_cols] + total[:ROWS]).astype(jnp.bfloat16)
-    slope_ref[...] = (wide[1, body, own_cols] + total[ROWS:]).astype(jnp.bfloat16)
+    out_ref[0] = (wide[0, body, own_cols] + total[:ROWS]).astype(jnp.bfloat16)
+    out_ref[1] = (wide[1, body, own_cols] + total[ROWS:]).astype(jnp.bfloat16)
 
     for j in range(own):
         drain(kv.at[j, pl.ds(0, 2 * ys * (xs - 1) + ys)], kv_send.at[j])
@@ -557,7 +558,7 @@
     sem = pltpu.SemaphoreType.DMA
     hbm = pl.BlockSpec(memory_space=pl.ANY)
     vmem = pl.BlockSpec(memory_space=pltpu.VMEM)
-    shape = jax.ShapeDtypeStruct((ROWS, half), jnp.bfloat16)
+    shape = jax.ShapeDtypeStruct((2, ROWS, half), jnp.bfloat16)
     operands = (
         frames,
         tangent,
@@ -571,11 +572,11 @@
         mix_weight,
     )
     part = (own, zs, 2 * HDIM + STAT, ys * ROWS)
-    return pl.pallas_call(
+    both = pl.pallas_call(
         functools.partial(kernel, sizes, heads),
-        out_shape=(shape, shape),
+        out_shape=shape,
         in_specs=[hbm] * len(operands),
-        out_specs=(vmem, vmem),
+        out_specs=vmem,
         scratch_shapes=[
             pltpu.VMEM((2, length, width), jnp.bfloat16),
             pltpu.VMEM((width,), jnp.float32),
@@ -621,6 +622,7 @@
         ),
         name="block",
     )(*operands)
+    return both[0], both[1]
 
 
 def solution(mesh):

time: 51.6 us -> 50.9 us (0.986)
  local copies, waits for them, and re-layouts: 2.22 us -> 1.64 us
    unnamed x4 -> x0, local copies, waits for them, and re-layouts: 2.22 us -> none
    squeeze x0 -> x1, local copies, waits for them, and re-layouts: none -> 1.64 us  [shards(): return (both[0], both[1])]
where the time goes in v5:
time: 50.9 us; the launch traced here: 50.8 us
  Pallas kernels  48.5 us (95%)
  local copies, waits for them, and re-layouts  1.64 us (3%)
  between operations  0.64 us (1%)
    pallas_call x1, Pallas kernels, shards(): pl.pallas_call(functools.partial(kernel, sizes, heads), out_shape=shape,...  48.5 us
    squeeze x1, local copies, waits for them, and re-layouts, shards(): return (both[0], both[1])  1.64 us

profile of v5, /device:TPU:1, one launch (start us, length us, event | category | flops | bytes accessed | tf_op | source)
XLA Modules:
  0.0 50.8 jit_solution(3790795180296388471)
XLA Ops:
  0.6 48.5 %block.1 = bf16[2,128,384]{2,1,0:T(8,128)(2,1)} custom-call(bf16[128,768]{1,0:T(8,128)(2,1)} %frames_hbm.1, bf16[128,768]{1,0:T(8,128)(2,1)} %tangent_hbm.1, f32[768]{0:T(1024)} %gain_hbm.1, bf16[768,384]{1,0:T(8,128)(2,1)} %wq_hbm.1, bf16[768,384]{1,0:T(8,128)(2,1)} %wk_hbm.1, bf16[768,384]{1,0:T(8,128)(2,1)} %wv_hbm.1, bf16[384,768]{1,0:T(8,128)(2,1)} %wo_hbm.1, ...), custom_call_target="tpu_custom_call" | custom-call | tf_op jit(solution)/shard_map/block/pallas_call | solution.py:575
  49.2 1.6 %slice_bitcast_fusion = (bf16[128,384]{1,0:T(8,128)(2,1)}, bf16[128,384]{1,0:T(8,128)(2,1)}) fusion(bf16[2,128,384]{2,1,0:T(8,128)(2,1)} %block.1), kind=kLoop, calls=%fused_computation | loop fusion | bytes 393216 | tf_op jit(solution)/shard_map/squeeze | solution.py:625

commit v6 on v5

--- a/solution.py
+++ b/solution.py
@@ -271,7 +271,7 @@
                 drain(kv.at[j, slot(other, core, which)], direct_recv.at[j, other, which])
             pass_on(j, other).start()
 
-    for j in range(own):
+    for j in range(own - 1):
         relay(j)
     forward(0)
     loads[6].wait()
@@ -442,6 +442,10 @@
             for step in range(xs):
                 source = lax.rem(x + step, xs)
                 drain(kv.at[j, pl.ds(slot(source, 1 - core, 0), ys)], sibling_recv.at[j, source])
+
+        @pl.when(u == min(2, own - 1))
+        def _():
+            relay(own - 1)
 
         @pl.when(jnp.logical_and(tile == max(zs - 2, 0), j < own - 1))
         def _():

time: 50.9 us -> 51.2 us (level)
  no operation moved by 1% of the time
where the time goes in v6:
time: 51.2 us; the launch traced here: 51 us
  Pallas kernels  48.7 us (95%)
  local copies, waits for them, and re-layouts  1.64 us (3%)
  between operations  0.64 us (1%)
    pallas_call x1, Pallas kernels, shards(): pl.pallas_call(functools.partial(kernel, sizes, heads), out_shape=shape,...  48.7 us
    squeeze x1, local copies, waits for them, and re-layouts, shards(): return (both[0], both[1])  1.64 us

profile of v6, /device:TPU:1, one launch (start us, length us, event | category | flops | bytes accessed | tf_op | source)
XLA Modules:
  0.0 51.0 jit_solution(15001981779466604089)
XLA Ops:
  0.6 48.7 %block.1 = bf16[2,128,384]{2,1,0:T(8,128)(2,1)} custom-call(bf16[128,768]{1,0:T(8,128)(2,1)} %frames_hbm.1, bf16[128,768]{1,0:T(8,128)(2,1)} %tangent_hbm.1, f32[768]{0:T(1024)} %gain_hbm.1, bf16[768,384]{1,0:T(8,128)(2,1)} %wq_hbm.1, bf16[768,384]{1,0:T(8,128)(2,1)} %wk_hbm.1, bf16[768,384]{1,0:T(8,128)(2,1)} %wv_hbm.1, bf16[384,768]{1,0:T(8,128)(2,1)} %wo_hbm.1, ...), custom_call_target="tpu_custom_call" | custom-call | tf_op jit(solution)/shard_map/block/pallas_call | solution.py:579
  49.4 1.6 %slice_bitcast_fusion = (bf16[128,384]{1,0:T(8,128)(2,1)}, bf16[128,384]{1,0:T(8,128)(2,1)}) fusion(bf16[2,128,384]{2,1,0:T(8,128)(2,1)} %block.1), kind=kLoop, calls=%fused_computation | loop fusion | bytes 393216 | tf_op jit(solution)/shard_map/squeeze | solution.py:629
